TPU v7x, 32 devices: a whole 2x2x4 slice. The times are simulated.
32 devices in a mesh: dp: 8 (over z, x), section: 2 (over y), tensor: 2 (over core).
Axes of the slice: x: 2, y: 2, z: 4, core: 2. Of those that a mesh axis runs over, the one named last changes fastest.
Arguments:
- own_rows: bfloat16 [2, 2048, 8192], P('section', 'dp', 'tensor'), may hold values from -6 to 6
- out_rows: bfloat16 [2, 2048, 28672], P('section', 'dp', 'tensor'), may hold values from -6 to 6
- val_own: bfloat16 [2, 1024, 8192], P('section', 'dp', 'tensor'), may hold values from -0.01171875 to 0.01171875
- val_out: bfloat16 [2, 1024, 28672], P('section', 'dp', 'tensor'), may hold values from -0.005859375 to 0.005859375
Outputs:
- token_scores: float32 [2048], P(('dp', 'tensor'))
- seq_scores: float32 [8], P('dp')
All inputs are finite; a program needn't handle non-finite values.
Results may differ from a plain program's by a relative error of at most 0.0003.
Values may be sent and summed in bfloat16 or wider, within the bound.
No kernel may reach another device: no remote copies, remote signals or barrier semaphores. Data moves between devices by JAX's collectives and lax.ppermute only.
A program may use at most 128 MiB of HBM per device.

v0:
```python
import jax
import jax.numpy as jnp
from jax import lax
from jax.sharding import PartitionSpec as P

LEN = 256


def swapped(x, axis, bit):
    return lax.ppermute(x, axis, [(i, i ^ 1 << bit) for i in range(lax.axis_size(axis))])


def row_gram(left_rows, right_rows):
    return lax.dot_general(
        left_rows, right_rows, (((1,), (1,)), ((), ())), preferred_element_type=jnp.float32
    )


def body(own_rows, out_rows, val_own, val_out):
    layer_input = own_rows[0]
    local_output = out_rows[0]
    val_input = val_own[0]
    val_output = val_out[0]
    token_count = layer_input.shape[0]
    paired_rows, paired_val = swapped((local_output, val_output), "section", 0)
    input_block = row_gram(layer_input, lax.all_gather(val_input, "dp", axis=0, tiled=True))
    output_block = row_gram(paired_rows, lax.all_gather(paired_val, "dp", axis=0, tiled=True))
    input_gram = input_block
    output_gram = output_block
    share_rows = token_count // lax.axis_size("tensor")
    input_gram, output_gram = (
        lax.psum_scatter(input_gram, "tensor", scatter_dimension=0, tiled=True),
        lax.psum_scatter(output_gram, "tensor", scatter_dimension=0, tiled=True),
    )
    layer_scores = jnp.sum(input_gram * output_gram, axis=1)
    token_scores = lax.psum(layer_scores, "section")
    row_index = lax.iota(jnp.int32, share_rows) + lax.axis_index("tensor") * share_rows
    member_mask = (row_index // LEN)[:, None] == lax.iota(jnp.int32, token_count // LEN)[None, :]
    seq_part = jnp.sum(jnp.where(member_mask, token_scores[:, None], jnp.float32(0.0)), axis=0)
    seq_scores = lax.psum(seq_part, "tensor")
    return (token_scores, seq_scores)


def solution(mesh):
    in_specs = (
        P("section", "dp", "tensor"),
        P("section", "dp", "tensor"),
        P("section", "dp", "tensor"),
        P("section", "dp", "tensor"),
    )
    out_specs = (P(("dp", "tensor")), P("dp"))
    return jax.shard_map(body, mesh=mesh, in_specs=in_specs, out_specs=out_specs, check_vma=False)
```

profile of v0, /device:TPU:0, one launch (start us, length us, event | category | flops | bytes accessed | tf_op | source)
XLA Modules:
  0.0 738.1 jit_solution(4401347163303793507)
XLA Ops:
  7.2 0.0 copy-start
  7.2 0.0 all-gather.6.cloned.1.call-start
  7.2 0.7 all-gather.6.cloned.1.call-update
  7.9 0.0 all-gather.4.cloned.1.call-start
  8.0 3.0 collective-permute-start.1
  11.0 79.7 %collective-permute-done.1 = bf16[128,14336]{1,0:T(8,128)(2,1)} collective-permute-done((bf16[128,14336]{1,0:T(8,128)(2,1)}, bf16[128,14336]{1,0:T(8,128)(2,1)}, u32[]{:S(2)}, u32[]{:S(2)}) %collective-permute-start.1) | collective-permute-done | bytes 3670048 | tf_op jit(solution)/shard_map/ppermute | solution.py:10
  90.6 0.0 all-gather.4.cloned.1.call-update
  90.7 0.0 reduce-scatter.3.cloned.1.call-start
  90.7 1.8 collective-permute-start
  92.5 45.3 %all-gather.6.cloned.1.call-done = bf16[1,1024,4096]{2,1,0:T(8,128)(2,1)} async-done(((bf16[1,128,4096]{2,1,0:T(8,128)(2,1)}), bf16[1,1024,4096]{2,1,0:T(8,128)(2,1)}) %all-gather.6.cloned.1.call-update) | async-done | bytes 8388624 | tf_op jit(solution)/shard_map/all_gather | solution.py:26
  137.8 0.0 copy-done
  137.8 6.7 fusion
  144.5 0.0 reduce-scatter.3.cloned.1.call-update
  144.5 0.0 reduce-scatter.5.cloned.1.call-start
  144.6 105.7 %collective-permute-done = bf16[256,14336]{1,0:T(8,128)(2,1)} collective-permute-done((bf16[256,14336]{1,0:T(8,128)(2,1)}, bf16[256,14336]{1,0:T(8,128)(2,1)}, u32[]{:S(2)}, u32[]{:S(2)}) %collective-permute-start) | collective-permute-done | bytes 7340064 | tf_op jit(solution)/shard_map/ppermute | solution.py:10
  250.3 446.4 %all-gather.4.cloned.1.call-done = bf16[1024,14336]{1,0:T(8,128)(2,1)} async-done(((bf16[128,14336]{1,0:T(8,128)(2,1)}), bf16[1024,14336]{1,0:T(8,128)(2,1)}) %all-gather.4.cloned.1.call-update) | async-done | bytes 29360144 | tf_op jit(solution)/shard_map/all_gather | solution.py:27
  696.6 16.1 %fusion.4 = f32[256,1024]{1,0:T(8,128)} fusion(bf16[256,14336]{1,0:T(8,128)(2,1)} %collective-permute-done, bf16[1024,14336]{1,0:T(8,128)(2,1)} %all-gather.4.cloned.1.call-done), kind=kOutput, calls=%fused_computation.10 | convolution fusion | flops 7516192768 | bytes 37748736 | tf_op jit(solution)/shard_map/dot_general | solution.py:14
  712.7 0.0 reduce-scatter.5.cloned.1.call-update
  712.7 0.0 reduce-scatter.3.cloned.1.call-done
  712.8 8.9 %reduce-scatter.5.cloned.1.call-done = f32[128,1024]{1,0:T(8,128)} async-done(((f32[256,1024]{1,0:T(8,128)}), f32[128,1024]{1,0:T(8,128)}) %reduce-scatter.5.cloned.1.call-update) | async-done | bytes 524304 | tf_op jit(solution)/shard_map/reduce_scatter | solution.py:33
  721.6 1.3 multiply_reduce_fusion
  723.0 4.9 psum.14
  727.9 0.0 copy-start.1
  727.9 0.6 fusion.3
  728.5 3.1 psum.15
  731.6 0.0 copy-done.1
Async XLA Ops:
  7.2 130.6 %copy-start = (bf16[1,256,4096]{2,1,0:T(8,128)(2,1)S(1)}, bf16[1,256,4096]{2,1,0:T(8,128)(2,1)}, u32[]{:S(2)}) copy-start(bf16[1,256,4096]{2,1,0:T(8,128)(2,1)} %param.4) | copy-start | bytes 6291460
  7.2 130.6 %all-gather.6.cloned.1.call-start = ((), (), s32[]{:S(2)}) async-start(), calls=%async_computation.5 | async-start | bytes 9437184 | tf_op jit(solution)/shard_map/all_gather | solution.py:26
  7.9 688.7 %all-gather.4.cloned.1.call-start = ((), (), s32[]{:S(2)}) async-start(), calls=%async_computation.3 | async-start | bytes 33030144 | tf_op jit(solution)/shard_map/all_gather | solution.py:27
  8.0 82.7 %collective-permute-start.1 = (bf16[128,14336]{1,0:T(8,128)(2,1)}, bf16[128,14336]{1,0:T(8,128)(2,1)}, u32[]{:S(2)}, u32[]{:S(2)}) collective-permute-start(bf16[128,14336]{1,0:T(8,128)(2,1)} %bitcast.12), channel_id=1, source_target_pairs={{0,2},{2,0},{1,3},{3,1},{4,6},{6,4},{5,7},{7,5},{8,10},{10,8},{9,1... | collective-permute-start | bytes 11010056 | tf_op jit(solution)/shard_map/ppermute | solution.py:10
  90.7 622.1 %reduce-scatter.3.cloned.1.call-start = ((), (), s32[]{:S(2)}) async-start(), calls=%async_computation.2 | async-start | bytes 1572864 | tf_op jit(solution)/shard_map/reduce_scatter | solution.py:32
  90.7 159.6 %collective-permute-start = (bf16[256,14336]{1,0:T(8,128)(2,1)}, bf16[256,14336]{1,0:T(8,128)(2,1)}, u32[]{:S(2)}, u32[]{:S(2)}) collective-permute-start(bf16[256,14336]{1,0:T(8,128)(2,1)} %bitcast.11), channel_id=1, source_target_pairs={{0,2},{2,0},{1,3},{3,1},{4,6},{6,4},{5,7},{7,5},{8,10},{10,8},{9,1... | collective-permute-start | bytes 22020104 | tf_op jit(solution)/shard_map/ppermute | solution.py:10
  144.5 577.1 %reduce-scatter.5.cloned.1.call-start = ((), (), s32[]{:S(2)}) async-start(), calls=%async_computation.4 | async-start | bytes 1572864 | tf_op jit(solution)/shard_map/reduce_scatter | solution.py:33
  727.9 3.7 copy-start.1
Sparse Core Ops, SparseCore 0:
  10.1 127.6 all-gather.5
  139.3 557.2 all-gather.3
  698.9 8.5 reduce-scatter.2
  712.9 8.7 reduce-scatter.4
where the time goes:
time: 738 us
  waiting for transfers between devices  687 us (93%)
  matrix products  22.8 us (3%)
  between operations  13.8 us (2%)
  blocking collectives  8.01 us (1%)
    all_gather x1, waiting for transfers between devices, body(): lax.all_gather(paired_val, 'dp', axis=0, tiled=True)  446 us
    ppermute x2, waiting for transfers between devices, swapped(): lax.ppermute(x, axis, [(i, i ^ 1 << bit) for i in range(lax.axis_size(axi...  185 us
    all_gather x1, waiting for transfers between devices, body(): lax.all_gather(val_input, 'dp', axis=0, tiled=True)  45.3 us
    dot_general x2, matrix products, row_gram(): lax.dot_general(left_rows, right_rows, (((1,), (1,)), ((), ())), preferre...  22.8 us
  transfers between devices with their start and end apart: 6, of which 5 were waited for; matrix products, arithmetic and copies ran while one was open for 3% of the time, Pallas kernels for 0%

commit v1 on v0

v1 whole, which is shorter than its diff:
```python
import jax
import jax.numpy as jnp
from jax import lax
from jax.sharding import Mesh, PartitionSpec as P

LEN = 256
SWAP = ((0, 1), (1, 0))


def row_gram(left_rows, right_rows):
    return lax.dot_general(
        left_rows, right_rows, (((1,), (1,)), ((), ())), preferred_element_type=jnp.float32
    )


def gate(x, after):
    return lax.optimization_barrier((x, after))[0]


def general(own_rows, out_rows, val_own, val_out):
    line = lax.axis_size("line")
    spot, side, core = lax.axis_index("line"), lax.axis_index("pair"), lax.axis_index("tensor")
    cores = lax.axis_size("tensor")
    own_rows, out_rows, val_own, val_out = own_rows[0], out_rows[0], val_own[0], val_out[0]
    rows, vals = own_rows.shape[0], val_own.shape[0]
    out_half = out_rows.shape[1] // 2
    handed = out_half * 13 // 28 // 128 * 128
    kept = out_half - handed
    upper = spot >= line // 2
    ends = [(0, 1), (line - 1, line - 2)]

    def split(array, at, size):
        low = lax.slice_in_dim(array, at, at + size, axis=1)
        high = lax.slice_in_dim(array, out_half + at, out_half + at + size, axis=1)
        return jnp.where(side == 0, low, high), jnp.where(side == 0, high, low)

    def across(x):
        return lax.ppermute(x, "pair", SWAP)

    def pairs(stage, is_handed):
        up = [(i, i + 1) for i in range(stage, line - 1)]
        if is_handed:
            up = up[:-1]
        return up, [(line - 1 - i, line - 1 - j) for i, j in up]

    def hop(x, stage, is_handed=False):
        up, down = pairs(stage, is_handed)
        return lax.ppermute(x[0], "line", up), lax.ppermute(x[1], "line", down)

    def middle(x):
        return jnp.where(upper, x[0], x[1])

    def hop_on(x, stage, is_handed=False):
        up, down = pairs(stage, is_handed)
        return lax.ppermute(x, "line", up + down)

    def joined(x, y):
        return tuple(jnp.concatenate(p, axis=0) for p in zip(x, y))

    v_kept, v_kept_far = split(val_out, 0, kept)
    own = {1: hop((val_own, val_own), 0)}
    v_kept_b = across(v_kept_far)
    kept_1a = hop((v_kept, v_kept), 0)
    half = line // 2
    for s in range(1, half):
        own[s + 1] = hop(own[s], s)
    v_hand, v_hand_far = split(gate(val_out, v_kept_b), kept, handed)
    v_hand_b = across(v_hand_far)
    x = gate(v_kept_b, kept_1a)
    kept_1b = hop((x, x), 0)
    t_own_b = across(gate(own_rows, v_hand_b))
    v_hand = jnp.concatenate((v_hand, v_hand_b))
    x = gate(v_hand, own[half])
    hand = {1: hop((x, x), 0, True)}
    kepts = {1: joined(kept_1a, kept_1b)}
    t_hand, t_hand_far = split(gate(out_rows, t_own_b), kept, handed)
    t_hand_b = across(t_hand_far)
    own[half] = middle(own[half])
    x = gate(own[half], kept_1b)
    for s in range(half, line - 1):
        x = own[s + 1] = hop_on(x, s)
    far_a = lax.ppermute(gate(t_hand, kept_1b), "line", ends)
    x = gate(kepts[1], own[line - 1])
    for s in range(1, half):
        x = kepts[s + 1] = hop(x, s)

    def entries(local, stages):
        out = [(0, 0, local)]
        for d, x in sorted(stages.items()):
            if isinstance(x, tuple):
                out += [(d, d, x[0]), (line - d, line - d, x[1])]
            else:
                out.append((d, line - d, x))
        return out

    t_own = jnp.concatenate((own_rows, t_own_b))
    blocks = [None] * line
    for ju, jl, v in entries(val_own, own):
        product = row_gram(t_own, v)
        for j, part in [(ju, product)] if ju == jl else [
            (ju, jnp.where(upper, product, 0.0)),
            (jl, jnp.where(upper, 0.0, product)),
        ]:
            blocks[j] = part if blocks[j] is None else blocks[j] + part
    part = jnp.concatenate(blocks, axis=1)

    def half_rows(x, which):
        return jnp.where(which == 0, x[:rows], x[rows:])

    share = half_rows(part, core) + lax.ppermute(half_rows(part, 1 - core), "tensor", SWAP)
    share = lax.ppermute(share, "section", SWAP)
    other = lax.ppermute(share, ("pair", "tensor"), [(i, 3 - i) for i in range(4)])
    share = jnp.concatenate((share.reshape(rows, line, vals), other.reshape(rows, line, vals)), axis=2)
    share = share.reshape(rows, line * 2 * vals)

    t_kept, t_kept_far = split(gate(out_rows, t_hand_b), 0, kept)
    t_kept_b = across(gate(t_kept_far, other))
    far_b = lax.ppermute(gate(t_hand_b, far_a), "line", ends)
    x = gate(hand[1], far_a)
    for s in range(1, half):
        x = hand[s + 1] = hop(x, s, True)
    x = kepts[half] = middle(kepts[half])
    for s in range(half, line - 1):
        x = kepts[s + 1] = hop_on(x, s)
    x = hand[half] = middle(hand[half])
    for s in range(half, line - 2):
        x = hand[s + 1] = hop_on(x, s, True)

    def both(share):
        twin = lax.ppermute(share, "tensor", SWAP)
        return jnp.concatenate((jnp.where(core == 0, share, twin), jnp.where(core == 0, twin, share)))

    def columns(x, j):
        return x[:, j * 2 * vals : (j + 1) * 2 * vals]

    def scores(grams, inputs):
        total = jnp.zeros((2 * rows,), jnp.float32)
        for (ju, jl), gram in grams.items():
            inp = inputs[ju] if ju == jl else jnp.where(upper, inputs[ju], inputs[jl])
            total = total + jnp.sum(inp * gram, axis=1)
        return total

    full = both(share)
    full = [columns(full, j) for j in range(line)]
    grams = {}
    t_kept = jnp.concatenate((t_kept, t_kept_b))
    for ju, jl, v in entries(jnp.concatenate((v_kept, v_kept_b)), kepts):
        grams[ju, jl] = row_gram(t_kept, v)
    hand_entries = entries(v_hand, hand)
    t_hand = jnp.concatenate((t_hand, t_hand_b))
    for ju, jl, v in hand_entries:
        grams[ju, jl] = grams[ju, jl] + row_gram(t_hand, v)
    t_far = jnp.concatenate((far_a, far_b))
    far_grams = {(ju, jl): row_gram(t_far, v) for ju, jl, v in hand_entries}
    far = both(lax.ppermute(share[:, 2 * vals :], "line", ends))
    far = [None] + [columns(far, j) for j in range(line - 1)]
    nothing = jnp.zeros_like(far[1])
    low_order, high_order = [nothing] * line, [nothing] * line
    for j in range(1, line):
        low_order[(j + 1) % line] = far[j]
        high_order[j - 1] = far[j]
    far_full = [jnp.where(upper, b, a) for a, b in zip(low_order, high_order)]

    return finish(scores(grams, full), scores(far_grams, far_full), rows, cores, core, ends)


def waves(own_rows, out_rows, val_own, val_out):
    line = lax.axis_size("line")
    spot, side, core = lax.axis_index("line"), lax.axis_index("pair"), lax.axis_index("tensor")
    cores = lax.axis_size("tensor")
    own_rows, out_rows, val_own, val_out = own_rows[0], out_rows[0], val_own[0], val_out[0]
    rows, vals = own_rows.shape[0], val_own.shape[0]
    out_half, wide = out_rows.shape[1] // 2, own_rows.shape[1]
    step = wide // 4
    last = line - 1
    upper = spot >= line // 2
    place = jnp.where(core == 0, spot, last - spot)
    far_side, low_end, high_end = place >= line // 2, place == 0, place == last
    end = low_end | high_end
    ends = [(0, 1), (last, last - 1)]
    sent, due = [], {}

    def split(array, at, size):
        low = lax.slice_in_dim(array, at, at + size, axis=1)
        high = lax.slice_in_dim(array, out_half + at, out_half + at + size, axis=1)
        return jnp.where(side == 0, low, high), jnp.where(side == 0, high, low)

    def along(x, pairs):
        n = len(sent)
        if n >= 3:
            x = gate(x, sent[n - 3])
        if n in due:
            x = gate(x, due[n])
        sent.append(lax.ppermute(x, ("line", "tensor"), pairs))
        return sent[-1]

    def across(x, after=None):
        return lax.ppermute(x if after is None else gate(x, after), "pair", SWAP)

    def wave(first, second, start=0):
        hops = [(i, i + 1) for i in range(start, last)]
        up = [(i * 2, j * 2) for i, j in hops] + [((last - i) * 2 + 1, (last - j) * 2 + 1) for i, j in hops]
        down = [(i * 2 + 1, j * 2 + 1) for i, j in hops] + [((last - i) * 2, (last - j) * 2) for i, j in hops]
        return along(first, up), along(second, down)

    def from_ends(x, received):
        return jnp.where(low_end, x, received[0]), jnp.where(high_end, x, received[1])

    def last_hop(x, held):
        return jnp.where(place == last - 1, held[0], x[0]), jnp.where(place == 1, held[1], x[1])

    def middle(x):
        return jnp.where(far_side, x[0], x[1])

    def other_way(x):
        return jnp.where(far_side, x[1], x[0])

    def flat(x):
        return jnp.concatenate((x[:vals], x[vals:]), axis=1)

    def stacked(x, parts):
        return jnp.concatenate(jnp.split(x, parts, axis=1), axis=0)

    kept, hand = wide, out_half - wide
    v_kept_a, v_kept_far = split(val_out, 0, kept)
    v_hand_a, v_hand_far = split(val_out, kept, hand)
    t_hand_a, t_hand_far = split(out_rows, kept, hand)
    t_kept_a, t_kept_far = split(out_rows, 0, kept)
    v_hand_b = across(v_hand_far)
    v_kept_b = across(v_kept_far)
    t_own_b = across(own_rows, v_hand_b)
    due[10] = t_own_b
    t_hand_b1 = across(t_hand_far[:, : 2 * step], t_own_b)
    t_hand_b2 = across(t_hand_far[:, 2 * step :], t_hand_b1)
    due[14] = t_hand_b2
    w0 = wave(val_own, val_own)
    w1 = wave(v_kept_a, v_kept_a)
    w2 = wave(*from_ends(flat(t_hand_a[:, : 2 * step]), w0))
    x = flat(t_hand_a[:, 2 * step :])
    w6 = wave(*from_ends(jnp.concatenate((x, x), axis=1), w1))
    hand_1 = jnp.concatenate((v_hand_a[:, : 2 * step], v_hand_b[:, : 2 * step]), axis=1)
    hand_2 = jnp.concatenate((v_hand_a[:, 2 * step :], v_hand_b[:, 2 * step :]), axis=1)
    w4 = wave(*last_hop((hand_1, hand_1), w2))

    t_own = jnp.concatenate((own_rows, t_own_b))
    far_own = middle(w4)
    cols = (val_own, jnp.where(low_end, far_own, w0[0]), middle(w2), jnp.where(high_end, far_own, w0[1]))
    block = jnp.split(row_gram(t_own, jnp.concatenate(cols)), line, axis=1)
    block[1], block[3] = jnp.where(core == 0, block[1], block[3]), jnp.where(core == 0, block[3], block[1])
    part = jnp.concatenate(block, axis=1)

    def half_rows(x, which):
        return jnp.where(which == 0, x[:rows], x[rows:])

    share = half_rows(part, core) + lax.ppermute(half_rows(part, 1 - core), "tensor", SWAP)
    due[12] = share
    share = lax.ppermute(share, "section", SWAP)
    due[16] = share
    t_kept_b1 = across(t_kept_far[:, : 2 * step], t_hand_b2)
    other = lax.ppermute(gate(share, t_kept_b1), ("pair", "tensor"), [(i, 3 - i) for i in range(4)])
    due[19] = other
    t_kept_b2 = across(t_kept_far[:, 2 * step :], other)
    share = jnp.concatenate((share.reshape(rows, line, vals), other.reshape(rows, line, vals)), axis=2)
    share = share.reshape(rows, line * 2 * vals)
    t_kept_b = jnp.concatenate((t_kept_b1, t_kept_b2), axis=1)
    far_share = lax.ppermute(share[:, 2 * vals :], "line", ends)
    w3 = wave(v_kept_b, v_kept_b)
    w5 = wave(*last_hop((hand_2, hand_2), [x[:, : 2 * step] for x in w6]))
    w7 = wave(*from_ends(flat(t_hand_b1), w3))
    w9 = wave(*last_hop(from_ends(flat(t_hand_b2), w5), [x[:, 2 * step :] for x in w6]))
    w8 = wave(*last_hop(w4, w7), 1)

    def both(share):
        twin = lax.ppermute(share, "tensor", SWAP)
        return jnp.concatenate((jnp.where(core == 0, share, twin), jnp.where(core == 0, twin, share)))

    def columns(x):
        return jnp.split(x, x.shape[1] // (2 * vals), axis=1)

    full = columns(both(share))
    full[1], full[3] = jnp.where(core == 0, full[1], full[3]), jnp.where(core == 0, full[3], full[1])
    far = columns(both(far_share))
    far_full = [
        jnp.where(upper, far[0], far[2]),
        jnp.where(far_side, far[1], 0.0),
        jnp.where(upper, far[2], far[0]),
        jnp.where(far_side, 0.0, far[1]),
    ]

    def kept_gram(a, b):
        return row_gram(t_kept, jnp.concatenate((a, b)))

    t_kept = jnp.concatenate((t_kept_a, t_kept_b))
    grams = [
        kept_gram(v_kept_a, v_kept_b),
        kept_gram(w1[0], w3[0]),
        kept_gram(middle(w6), middle(w7)),
        kept_gram(w1[1], w3[1]),
    ]
    last_gram = kept_gram(jnp.concatenate((middle(w5), middle(w9)), axis=1), middle(w8))
    t_hand_b = jnp.concatenate((t_hand_b1, t_hand_b2), axis=1)
    t_hand = jnp.concatenate((t_hand_a, t_hand_b))
    far_1 = jnp.concatenate((stacked(other_way(w2), 2), stacked(other_way(w7), 2)))
    far_2 = jnp.concatenate((stacked(other_way(w6)[:, : 2 * step], 2), stacked(other_way(w9), 2)))
    hand_rows = [(hand_1, hand_2), (w4[0], w5[0]), (middle(w8), middle(w9)), (w4[1], w5[1])]
    unused = [None, high_end, end, low_end]
    far_grams = []
    for j, (one, two) in enumerate(hand_rows):
        one, two = stacked(one, 2), stacked(two, 2)
        gram = row_gram(t_hand[:, : 2 * step], one) + row_gram(t_hand[:, 2 * step :], two)
        if j:
            gram = jnp.where(unused[j], 0.0, gram)
        grams[j] = grams[j] + gram
        far_grams.append(row_gram(far_1, one) + row_gram(far_2, two))
    last_inputs = jnp.where(end, jnp.where(far_side, full[3], full[1]), 0.0)
    score = jnp.sum(sum(x * y for x, y in zip(full + [last_inputs], grams + [last_gram])), axis=1)
    far_score = jnp.sum(sum(x * y for x, y in zip(far_full, far_grams)), axis=1)
    return finish(score, far_score, rows, cores, core, ends)


def finish(score, far_score, rows, cores, core, ends):
    sums = jnp.concatenate((score, far_score))
    sums = sums + lax.ppermute(sums, "tensor", SWAP)
    sums = sums + lax.ppermute(sums, "section", SWAP)
    a, b, far_a, far_b = (sums[i * rows : (i + 1) * rows] for i in range(4))
    back = [(j, i) for i, j in ends]
    mine = a + lax.ppermute(b, "pair", SWAP) + lax.ppermute(far_a, "line", back)
    slanted = [(j * 2 + s, i * 2 + 1 - s) for i, j in ends for s in range(2)]
    mine = mine + lax.ppermute(far_b, ("line", "pair"), slanted)
    token_count = rows // cores
    token_scores = lax.dynamic_slice_in_dim(mine, core * token_count, token_count)
    seq_scores = jnp.sum(mine.reshape(rows // LEN, LEN), axis=1)
    return token_scores, seq_scores


def body(own_rows, out_rows, val_own, val_out):
    rows, vals = own_rows.shape[1], val_own.shape[1]
    fits = rows == 2 * vals and out_rows.shape[2] * 2 == own_rows.shape[2] * 7
    if lax.axis_size("line") == 4 and lax.axis_size("tensor") == 2 and fits:
        return waves(own_rows, out_rows, val_own, val_out)
    return general(own_rows, out_rows, val_own, val_out)


def solution(mesh):
    dp, section, tensor = (mesh.shape[name] for name in ("dp", "section", "tensor"))
    names = ("line", "pair", "section", "tensor")
    split = Mesh(mesh.devices.reshape(dp // 2, 2, section, tensor), names)
    in_specs = (P("section", ("line", "pair"), "tensor"),) * 4
    out_specs = (P(("line", "pair", "tensor")), P(("line", "pair")))
    return jax.shard_map(body, mesh=split, in_specs=in_specs, out_specs=out_specs, check_vma=False)
```

time: 738 us -> 252 us (0.34)
  waiting for transfers between devices: 687 us -> 111 us
  starting transfers between devices: 4.99 us -> 79.2 us
  other arithmetic: 1.94 us -> 21.1 us
  between operations: 13.8 us -> 1.46 us
  local copies, waits for them, and re-layouts: 0.01 us -> 11.8 us
  blocking collectives: 8.01 us -> 0 us
    all_gather x2 -> x0, waiting for transfers between devices: 492 us -> none  [the longest x1 446 us: body(): lax.all_gather(paired_val, 'dp', axis=0, tiled=True)]
    ppermute x2 -> x38, starting transfers between devices: 4.84 us -> 79.2 us  [the longest x20 54.4 us: along(): sent.append(lax.ppermute(x, ('line', 'tensor'), pairs))]
    ppermute x2 -> x38, waiting for transfers between devices: 185 us -> 111 us  [the longest x20 42.8 us: along(): sent.append(lax.ppermute(x, ('line', 'tensor'), pairs))]
    select_n x0 -> x18, other arithmetic: none -> 19.9 us  [the longest x4 7.69 us: split(): return (jnp.where(side == 0, low, high), jnp.where(side == 0, high, low))]
    slice x0 -> x13, local copies, waits for them, and re-layouts: none -> 10.5 us  [the longest x4 2.03 us: flat(): return jnp.concatenate((x[:vals], x[vals:]), axis=1)]
    reduce_scatter x2 -> x0, waiting for transfers between devices: 8.89 us -> none  [the longest x1 8.87 us: body(): lax.psum_scatter(output_gram, 'tensor', scatter_dimension=0, tiled=True)]
    psum x2 -> x0, blocking collectives: 8.01 us -> none  [the longest x1 4.94 us: body(): token_scores = lax.psum(layer_scores, 'section')]
    dot_general x2 -> x22, matrix products: 22.8 us -> 26 us  [row_gram(): lax.dot_general(left_rows, right_rows, (((1,), (1,)), ((), ())), preferre...]
  transfers between devices with their start and end apart: 6 -> 38, of which waited for: 5 -> 16; matrix products, arithmetic and copies ran while one was open for 3% -> 23% of each run, Pallas kernels for 0% -> 0%
where the time goes in v1:
time: 252 us; the launch traced here: 251 us
  waiting for transfers between devices  111 us (44%)
  starting transfers between devices  79.2 us (31%)
  matrix products  26 us (10%)
  other arithmetic  21.1 us (8%)
  local copies, waits for them, and re-layouts  11.8 us (5%)
    ppermute x20, starting transfers between devices, along(): sent.append(lax.ppermute(x, ('line', 'tensor'), pairs))  54.4 us
    ppermute x20, waiting for transfers between devices, along(): sent.append(lax.ppermute(x, ('line', 'tensor'), pairs))  42.8 us
    ppermute x7, waiting for transfers between devices, across(): return lax.ppermute(x if after is None else gate(x, after), 'pair', SWAP)  41.1 us
    dot_general x22, matrix products, row_gram(): lax.dot_general(left_rows, right_rows, (((1,), (1,)), ((), ())), preferre...  26 us
    ppermute x1, waiting for transfers between devices, waves(): far_share = lax.ppermute(share[:, 2 * vals:], 'line', ends)  9.72 us
    ppermute x1, waiting for transfers between devices, waves(): lax.ppermute(gate(share, t_kept_b1), ('pair', 'tensor'), [(i, 3 - i) for...  9.64 us
    ppermute x7, starting transfers between devices, across(): return lax.ppermute(x if after is None else gate(x, after), 'pair', SWAP)  9.46 us
    select_n x4, other arithmetic, split(): return (jnp.where(side == 0, low, high), jnp.where(side == 0, high, low))  7.69 us
  transfers between devices with their start and end apart: 38, of which 16 were waited for; matrix products, arithmetic and copies ran while one was open for 23% of the time, Pallas kernels for 0%

profile of v1, /device:TPU:0, one launch (start us, length us, event | category | flops | bytes accessed | tf_op | source)
XLA Modules:
  0.0 250.6 jit_solution(15868356799710118288)
XLA Ops:
  1.9 6.6 %collective-permute-start.2 = (bf16[128,4096]{1,0:T(8,128)(2,1)}, bf16[128,4096]{1,0:T(8,128)(2,1)}, u32[]{:S(2)}, u32[]{:S(2)}) collective-permute-start(bf16[128,4096]{1,0:T(8,128)(2,1)} %bitcast.25), channel_id=1, source_target_pairs={{0,8},{8,16},{16,24},{25,17},{17,9},{9,1},{2,10},{10,18},{18,26},{... | collective-permute-start | bytes 3145736 | tf_op jit(solution)/shard_map/ppermute | solution.py:194
  8.6 2.8 %broadcast_select_fusion.26 = (bf16[128,3072]{1,0:T(8,128)(2,1)}, bf16[128,3072]{1,0:T(8,128)(2,1)}) fusion(pred[]{:T(512)S(6)} %eq.15, bf16[128,14336]{1,0:T(8,128)(2,1)} %bitcast.18), kind=kLoop, calls=%fused_computation.110 | loop fusion | flops 786432 | bytes 3145729 | tf_op jit(solution)/shard_map/jit(_where)/select_n | solution.py:186
  11.3 1.9 collective-permute-start
  13.3 3.1 %broadcast_select_fusion.6 = (bf16[128,4096]{1,0:T(8,128)(2,1)}, bf16[128,4096]{1,0:T(8,128)(2,1)}) fusion(pred[]{:T(512)S(6)} %eq.15, bf16[128,14336]{1,0:T(8,128)(2,1)} %bitcast.19), kind=kLoop, calls=%fused_computation.90 | loop fusion | flops 1048576 | bytes 4194305 | tf_op jit(solution)/shard_map/jit(_where)/select_n | solution.py:186
  16.7 3.6 %collective-permute-start.5 = (bf16[128,4096]{1,0:T(8,128)(2,1)}, bf16[128,4096]{1,0:T(8,128)(2,1)}, u32[]{:S(2)}, u32[]{:S(2)}) collective-permute-start(bf16[128,4096]{1,0:T(8,128)(2,1)} %get-tuple-element.34), channel_id=1, source_target_pairs={{0,8},{8,16},{16,24},{25,17},{17,9},{9,1},{2,10},{10,18},{18,26},{... | collective-permute-start | bytes 3145736 | tf_op jit(solution)/shard_map/ppermute | solution.py:194
  20.4 1.6 broadcast_select_fusion
  22.2 1.6 fusion.131
  24.8 3.5 %collective-permute-done.2 = bf16[128,4096]{1,0:T(8,128)(2,1)} collective-permute-done((bf16[128,4096]{1,0:T(8,128)(2,1)}, bf16[128,4096]{1,0:T(8,128)(2,1)}, u32[]{:S(2)}, u32[]{:S(2)}) %collective-permute-start.2) | collective-permute-done | bytes 1048608 | tf_op jit(solution)/shard_map/ppermute | solution.py:194
  29.6 3.5 %broadcast_select_fusion.25 = (bf16[128,4096]{1,0:T(8,128)(2,1)}, bf16[128,4096]{1,0:T(8,128)(2,1)}) fusion(bf16[128,4096]{1,0:T(8,128)(2,1)} %collective-permute-done.2, pred[]{:T(512)S(6)} %eq.16, bf16[128,2048]{1,0:T(8,128)(2,1)} %get-tuple-element.83, bf16[128,2048]{1,0:T(8,128)(2,1)} %get-tuple-element.82, ...), kind=kLoop, calls=%fused_computation.109 | loop fusion | flops 3145728 | bytes 5242882 | tf_op jit(solution)/shard_map/jit(_where)/select_n | solution.py:207
  33.1 11.5 %collective-permute-done.5 = bf16[128,4096]{1,0:T(8,128)(2,1)} collective-permute-done((bf16[128,4096]{1,0:T(8,128)(2,1)}, bf16[128,4096]{1,0:T(8,128)(2,1)}, u32[]{:S(2)}, u32[]{:S(2)}) %collective-permute-start.5) | collective-permute-done | bytes 1048608 | tf_op jit(solution)/shard_map/ppermute | solution.py:194
  45.9 6.0 %collective-permute-start.4 = (bf16[128,4096]{1,0:T(8,128)(2,1)}, bf16[128,4096]{1,0:T(8,128)(2,1)}, u32[]{:S(2)}, u32[]{:S(2)}) collective-permute-start(bf16[128,4096]{1,0:T(8,128)(2,1)} %get-tuple-element.31), channel_id=1, source_target_pairs={{0,8},{8,16},{16,24},{25,17},{17,9},{9,1},{2,10},{10,18},{18,26},{... | collective-permute-start | bytes 3145736 | tf_op jit(solution)/shard_map/ppermute | solution.py:194
  53.7 1.9 slice.171
  57.5 1.5 collective-permute-start.1
  61.1 2.2 broadcast_select_fusion.9
  63.3 11.3 %collective-permute-done.4 = bf16[128,4096]{1,0:T(8,128)(2,1)} collective-permute-done((bf16[128,4096]{1,0:T(8,128)(2,1)}, bf16[128,4096]{1,0:T(8,128)(2,1)}, u32[]{:S(2)}, u32[]{:S(2)}) %collective-permute-start.4) | collective-permute-done | bytes 1048608 | tf_op jit(solution)/shard_map/ppermute | solution.py:194
  74.6 4.4 %collective-permute-start.9 = (bf16[128,4096]{1,0:T(8,128)(2,1)S(1)}, bf16[128,4096]{1,0:T(8,128)(2,1)S(1)}, u32[]{:S(2)}, u32[]{:S(2)}) collective-permute-start(bf16[128,4096]{1,0:T(8,128)(2,1)S(1)} %get-tuple-element.35), channel_id=1, source_target_pairs={{0,8},{8,16},{16,24},{25,17},{17,9},{9,1},{2,10},{10,18},{18,26},{... | collective-permute-start | bytes 3145736 | tf_op jit(solution)/shard_map/ppermute | solution.py:194
  80.3 2.5 broadcast_select_fusion.16
  82.9 4.7 %collective-permute-start.7 = (bf16[128,4096]{1,0:T(8,128)(2,1)S(1)}, bf16[128,4096]{1,0:T(8,128)(2,1)S(1)}, u32[]{:S(2)}, u32[]{:S(2)}) collective-permute-start(bf16[128,4096]{1,0:T(8,128)(2,1)S(1)} %get-tuple-element.33), channel_id=1, source_target_pairs={{0,8},{8,16},{16,24},{25,17},{17,9},{9,1},{2,10},{10,18},{18,26},{... | collective-permute-start | bytes 3145736 | tf_op jit(solution)/shard_map/ppermute | solution.py:194
  87.7 17.8 %collective-permute-done.1 = bf16[256,4096]{1,0:T(8,128)(2,1)S(1)} collective-permute-done((bf16[256,4096]{1,0:T(8,128)(2,1)}, bf16[256,4096]{1,0:T(8,128)(2,1)S(1)}, u32[]{:S(2)}, u32[]{:S(2)}) %collective-permute-start.1) | collective-permute-done | bytes 2097184 | tf_op jit(solution)/shard_map/ppermute | solution.py:198
  105.5 1.5 collective-permute-start.13
  107.0 3.5 %collective-permute-start.21 = (bf16[128,4096]{1,0:T(8,128)(2,1)}, bf16[128,4096]{1,0:T(8,128)(2,1)S(1)}, u32[]{:S(2)}, u32[]{:S(2)}) collective-permute-start(bf16[128,4096]{1,0:T(8,128)(2,1)} %collective-permute-done.19), channel_id=1, source_target_pairs={{0,8},{8,16},{16,24},{25,17},{17,9},{9,1},{2,10},{10,18},{18,26},{... | collective-permute-start | bytes 3145736 | tf_op jit(solution)/shard_map/ppermute | solution.py:194
  110.7 1.4 collective-permute-start.10
  112.2 1.6 collective-permute-done.7
  115.4 16.0 %collective-permute-done.13 = bf16[256,2048]{1,0:T(8,128)(2,1)S(1)} collective-permute-done((bf16[256,2048]{1,0:T(8,128)(2,1)S(1)}, bf16[256,2048]{1,0:T(8,128)(2,1)S(1)}, u32[]{:S(2)}, u32[]{:S(2)}) %collective-permute-start.13) | collective-permute-done | bytes 1048608 | tf_op jit(solution)/shard_map/ppermute | solution.py:198
  131.4 1.5 collective-permute-start.14
  133.0 3.4 %collective-permute-done.21 = bf16[128,4096]{1,0:T(8,128)(2,1)S(1)} collective-permute-done((bf16[128,4096]{1,0:T(8,128)(2,1)}, bf16[128,4096]{1,0:T(8,128)(2,1)S(1)}, u32[]{:S(2)}, u32[]{:S(2)}) %collective-permute-start.21) | collective-permute-done | bytes 1048608 | tf_op jit(solution)/shard_map/ppermute | solution.py:194
  137.7 1.5 broadcast_select_fusion.23
  139.2 4.6 %fusion = f32[512,512]{0,1:T(8,128)S(1)} fusion(bf16[256,4096]{1,0:T(8,128)(2,1)} %copy-done.7, bf16[256,4096]{1,0:T(8,128)(2,1)} %bitcast.23, bf16[128,4096]{1,0:T(8,128)(2,1)S(1)} %get-tuple-element.79, bf16[128,4096]{1,0:T(8,128)(2,1)S(1)} %get-tuple-element.77, bf16[128,4096]{1,0:T(8,128)(2,1)S(1)} %get-tuple-element.78, bf16[128,4096]{1,0:T(8,128)(2,1)S(1)} %bitcast.26), kind=kOutput, calls=%fused_computation | convolution fusion | flops 2172649472 | bytes 9437184 | tf_op jit(solution)/shard_map/dot_general | solution.py:11
  144.1 3.0 %collective-permute-done.23 = bf16[128,4096]{1,0:T(8,128)(2,1)S(1)} collective-permute-done((bf16[128,4096]{1,0:T(8,128)(2,1)}, bf16[128,4096]{1,0:T(8,128)(2,1)S(1)}, u32[]{:S(2)}, u32[]{:S(2)}) %collective-permute-start.23) | collective-permute-done | bytes 1048608 | tf_op jit(solution)/shard_map/ppermute | solution.py:194
  148.4 3.7 %collective-permute-start.24 = (bf16[128,4096]{1,0:T(8,128)(2,1)S(1)}, bf16[128,4096]{1,0:T(8,128)(2,1)S(1)}, u32[]{:S(2)}, u32[]{:S(2)}) collective-permute-start(bf16[128,4096]{1,0:T(8,128)(2,1)S(1)} %get-tuple-element.49), channel_id=1, source_target_pairs={{0,8},{8,16},{16,24},{25,17},{17,9},{9,1},{2,10},{10,18},{18,26},{... | collective-permute-start | bytes 3145736 | tf_op jit(solution)/shard_map/ppermute | solution.py:194
  152.2 1.6 collective-permute-start.15
  154.9 1.6 collective-permute-start.12
  156.5 3.6 %collective-permute-start.22 = (bf16[128,2048]{1,0:T(8,128)(2,1)S(1)}, bf16[128,2048]{1,0:T(8,128)(2,1)S(1)}, u32[]{:S(2)}, u32[]{:S(2)}) collective-permute-start(bf16[128,2048]{1,0:T(8,128)(2,1)S(1)} %get-tuple-element.46), channel_id=1, source_target_pairs={{0,8},{8,16},{16,24},{25,17},{17,9},{9,1},{2,10},{10,18},{18,26},{... | collective-permute-start | bytes 1572872 | tf_op jit(solution)/shard_map/ppermute | solution.py:194
  161.4 8.6 %collective-permute-done.22 = bf16[128,2048]{1,0:T(8,128)(2,1)S(1)} collective-permute-done((bf16[128,2048]{1,0:T(8,128)(2,1)S(1)}, bf16[128,2048]{1,0:T(8,128)(2,1)S(1)}, u32[]{:S(2)}, u32[]{:S(2)}) %collective-permute-start.22) | collective-permute-done | bytes 524320 | tf_op jit(solution)/shard_map/ppermute | solution.py:194
  170.6 4.4 %collective-permute-start.28 = (bf16[128,2048]{1,0:T(8,128)(2,1)S(1)}, bf16[128,2048]{1,0:T(8,128)(2,1)S(1)}, u32[]{:S(2)}, u32[]{:S(2)}) collective-permute-start(bf16[128,2048]{1,0:T(8,128)(2,1)S(1)} %get-tuple-element.54), channel_id=1, source_target_pairs={{0,8},{8,16},{16,24},{25,17},{17,9},{9,1},{2,10},{10,18},{18,26},{... | collective-permute-start | bytes 1572872 | tf_op jit(solution)/shard_map/ppermute | solution.py:194
  177.7 3.9 %collective-permute-start.16 = (f32[256,512]{0,1:T(8,128)S(1)}, f32[256,512]{0,1:T(8,128)S(1)}, u32[]{:S(2)}, u32[]{:S(2)}) collective-permute-start(f32[256,512]{0,1:T(8,128)S(1)} %collective-permute-done.12), channel_id=1, source_target_pairs={{0,5},{1,4},{4,1},{5,0},{2,7},{3,6},{6,3},{7,2},{8,13},{9,12},{12,... | collective-permute-start | bytes 1572872 | tf_op jit(solution)/shard_map/ppermute | solution.py:260
  182.1 1.6 fusion.59
  183.6 9.6 %collective-permute-done.16 = f32[256,512]{0,1:T(8,128)S(1)} collective-permute-done((f32[256,512]{0,1:T(8,128)S(1)}, f32[256,512]{0,1:T(8,128)S(1)}, u32[]{:S(2)}, u32[]{:S(2)}) %collective-permute-start.16) | collective-permute-done | bytes 524320 | tf_op jit(solution)/shard_map/ppermute | solution.py:260
  194.4 3.5 %collective-permute-start.31 = (f32[256,768]{0,1:T(8,128)S(1)}, f32[256,768]{0,1:T(8,128)S(1)}, u32[]{:S(2)}, u32[]{:S(2)}) collective-permute-start(f32[256,768]{0,1:T(8,128)S(1)} %slice.196), channel_id=1, source_target_pairs={{0,8},{24,16},{1,9},{25,17},{2,10},{26,18},{3,11},{27,19},{4,12},{... | collective-permute-start | bytes 2359304 | tf_op jit(solution)/shard_map/ppermute | solution.py:266
  205.6 9.7 %collective-permute-done.31 = f32[256,768]{0,1:T(8,128)S(1)} collective-permute-done((f32[256,768]{0,1:T(8,128)S(1)}, f32[256,768]{0,1:T(8,128)S(1)}, u32[]{:S(2)}, u32[]{:S(2)}) %collective-permute-start.31) | collective-permute-done | bytes 786464 | tf_op jit(solution)/shard_map/ppermute | solution.py:266
  215.5 7.3 %collective-permute-done.18 = bf16[256,2048]{1,0:T(8,128)(2,1)S(1)} collective-permute-done((bf16[256,2048]{1,0:T(8,128)(2,1)S(1)}, bf16[256,2048]{1,0:T(8,128)(2,1)S(1)}, u32[]{:S(2)}, u32[]{:S(2)}) %collective-permute-start.18) | collective-permute-done | bytes 1048608 | tf_op jit(solution)/shard_map/ppermute | solution.py:198
  222.8 2.5 %fusion.77 = f32[512,256]{0,1:T(8,128)S(1)} fusion(f32[512,256]{0,1:T(8,128)S(1)} %copy-done.9, bf16[128,4096]{1,0:T(8,128)(2,1)S(1)} %collective-permute-done.21, bf16[128,4096]{1,0:T(8,128)(2,1)} %collective-permute-done.5, pred[]{:T(512)S(6)} %eq.14, f32[256,1024]{0,1:T(8,128)S(1)} %get-tuple-element.75, f32[256,1024]{0,1:T(8,128)S(1)} %get-tuple-element.74, ...), kind=kOutput, calls=%fused_computation.74 | convolution fusion | flops 1091174400 | bytes 9437185 | tf_op jit(solution)/shard_map/dot_general | solution.py:11
  225.3 2.8 %fusion.80 = f32[512,256]{0,1:T(8,128)S(1)} fusion(f32[512,256]{0,1:T(8,128)S(1)} %fusion.41, bf16[128,4096]{1,0:T(8,128)(2,1)} %collective-permute-done.19, bf16[128,4096]{1,0:T(8,128)(2,1)} %get-tuple-element.34, bf16[256,2048]{1,0:T(8,128)(2,1)S(1)} %collective-permute-done.18, bf16[256,2048]{1,0:T(8,128)(2,1)S(1)} %collective-permute-done.15, ...), kind=kOutput, calls=%fused_computation.75 | convolution fusion | flops 1090650112 | bytes 7340032 | tf_op jit(solution)/shard_map/dot_general | solution.py:11
  228.2 2.5 %fusion.68 = f32[512,256]{0,1:T(8,128)S(1)} fusion(f32[512,256]{0,1:T(8,128)S(1)} %fusion.53, bf16[128,4096]{1,0:T(8,128)(2,1)S(1)} %collective-permute-done.23, bf16[128,4096]{1,0:T(8,128)(2,1)} %collective-permute-done.8, pred[]{:T(512)S(6)} %eq.14, f32[256,1024]{0,1:T(8,128)S(1)} %get-tuple-element.75, f32[256,1024]{0,1:T(8,128)S(1)} %get-tuple-element.74, ...), kind=kOutput, calls=%fused_computation.71 | convolution fusion | flops 1091174400 | bytes 9437185 | tf_op jit(solution)/shard_map/dot_general | solution.py:11
  233.9 1.4 fusion.96
  237.5 1.5 collective-permute-start.34
  239.0 2.1 collective-permute-done.34
  244.9 3.8 %collective-permute-done.37 = f32[256]{0:T(256)S(1)} collective-permute-done((f32[256]{0:T(256)S(1)}, f32[256]{0:T(256)S(1)}, u32[]{:S(2)}, u32[]{:S(2)}) %collective-permute-start.37) | collective-permute-done | bytes 1056 | tf_op jit(solution)/shard_map/ppermute | solution.py:329
  (121 shorter events, 43.4 us)
Async XLA Ops:
  0.6 28.9 %collective-permute-start.3 = (bf16[128,4096]{1,0:T(8,128)(2,1)}, bf16[128,4096]{1,0:T(8,128)(2,1)}, u32[]{:S(2)}, u32[]{:S(2)}) collective-permute-start(bf16[128,4096]{1,0:T(8,128)(2,1)} %bitcast.24), channel_id=1, source_target_pairs={{1,9},{9,17},{17,25},{24,16},{16,8},{8,0},{3,11},{11,19},{19,27},{... | collective-permute-start | bytes 3145736 | tf_op jit(solution)/shard_map/ppermute | solution.py:194
  1.9 26.4 %collective-permute-start.2 = (bf16[128,4096]{1,0:T(8,128)(2,1)}, bf16[128,4096]{1,0:T(8,128)(2,1)}, u32[]{:S(2)}, u32[]{:S(2)}) collective-permute-start(bf16[128,4096]{1,0:T(8,128)(2,1)} %bitcast.25), channel_id=1, source_target_pairs={{0,8},{8,16},{16,24},{25,17},{17,9},{9,1},{2,10},{10,18},{18,26},{... | collective-permute-start | bytes 3145736 | tf_op jit(solution)/shard_map/ppermute | solution.py:194
  8.6 11.8 %copy-start = (bf16[1,256,14336]{2,1,0:T(8,128)(2,1)S(1)}, bf16[1,256,14336]{2,1,0:T(8,128)(2,1)}, u32[]{:S(2)}) copy-start(bf16[1,256,14336]{2,1,0:T(8,128)(2,1)} %param.5) | copy-start | bytes 22020100
  11.3 46.2 %collective-permute-start = (bf16[128,3072]{1,0:T(8,128)(2,1)}, bf16[128,3072]{1,0:T(8,128)(2,1)}, u32[]{:S(2)}, u32[]{:S(2)}) collective-permute-start(bf16[128,3072]{1,0:T(8,128)(2,1)} %get-tuple-element.67), channel_id=1, source_target_pairs={{0,4},{4,0},{1,5},{5,1},{2,6},{6,2},{3,7},{7,3},{8,12},{12,8},{9,1... | collective-permute-start | bytes 2359304 | tf_op jit(solution)/shard_map/ppermute | solution.py:198
  16.4 90.6 %collective-permute-start.19 = (bf16[128,4096]{1,0:T(8,128)(2,1)}, bf16[128,4096]{1,0:T(8,128)(2,1)}, u32[]{:S(2)}, u32[]{:S(2)}) collective-permute-start(bf16[128,4096]{1,0:T(8,128)(2,1)} %get-tuple-element.64), channel_id=1, source_target_pairs={{0,4},{4,0},{1,5},{5,1},{2,6},{6,2},{3,7},{7,3},{8,12},{12,8},{9,1... | collective-permute-start | bytes 3145736 | tf_op jit(solution)/shard_map/ppermute | solution.py:198
  16.7 27.9 %collective-permute-start.5 = (bf16[128,4096]{1,0:T(8,128)(2,1)}, bf16[128,4096]{1,0:T(8,128)(2,1)}, u32[]{:S(2)}, u32[]{:S(2)}) collective-permute-start(bf16[128,4096]{1,0:T(8,128)(2,1)} %get-tuple-element.34), channel_id=1, source_target_pairs={{0,8},{8,16},{16,24},{25,17},{17,9},{9,1},{2,10},{10,18},{18,26},{... | collective-permute-start | bytes 3145736 | tf_op jit(solution)/shard_map/ppermute | solution.py:194
  28.3 32.8 %collective-permute-start.8 = (bf16[128,4096]{1,0:T(8,128)(2,1)}, bf16[128,4096]{1,0:T(8,128)(2,1)}, u32[]{:S(2)}, u32[]{:S(2)}) collective-permute-start(bf16[128,4096]{1,0:T(8,128)(2,1)} %get-tuple-element.34), channel_id=1, source_target_pairs={{1,9},{9,17},{17,25},{24,16},{16,8},{8,0},{3,11},{11,19},{19,27},{... | collective-permute-start | bytes 3145736 | tf_op jit(solution)/shard_map/ppermute | solution.py:194
  44.6 35.7 %collective-permute-start.6 = (bf16[128,4096]{1,0:T(8,128)(2,1)}, bf16[128,4096]{1,0:T(8,128)(2,1)}, u32[]{:S(2)}, u32[]{:S(2)}) collective-permute-start(bf16[128,4096]{1,0:T(8,128)(2,1)} %get-tuple-element.32), channel_id=1, source_target_pairs={{1,9},{9,17},{17,25},{24,16},{16,8},{8,0},{3,11},{11,19},{19,27},{... | collective-permute-start | bytes 3145736 | tf_op jit(solution)/shard_map/ppermute | solution.py:194
  45.9 28.6 %collective-permute-start.4 = (bf16[128,4096]{1,0:T(8,128)(2,1)}, bf16[128,4096]{1,0:T(8,128)(2,1)}, u32[]{:S(2)}, u32[]{:S(2)}) collective-permute-start(bf16[128,4096]{1,0:T(8,128)(2,1)} %get-tuple-element.31), channel_id=1, source_target_pairs={{0,8},{8,16},{16,24},{25,17},{17,9},{9,1},{2,10},{10,18},{18,26},{... | collective-permute-start | bytes 3145736 | tf_op jit(solution)/shard_map/ppermute | solution.py:194
  57.5 48.0 %collective-permute-start.1 = (bf16[256,4096]{1,0:T(8,128)(2,1)}, bf16[256,4096]{1,0:T(8,128)(2,1)S(1)}, u32[]{:S(2)}, u32[]{:S(2)}) collective-permute-start(bf16[256,4096]{1,0:T(8,128)(2,1)} %bitcast.22), channel_id=1, source_target_pairs={{0,4},{4,0},{1,5},{5,1},{2,6},{6,2},{3,7},{7,3},{8,12},{12,8},{9,1... | collective-permute-start | bytes 6291464 | tf_op jit(solution)/shard_map/ppermute | solution.py:198
  61.1 19.3 %copy-start.2 = (bf16[128,2048]{1,0:T(8,128)(2,1)S(1)}, bf16[128,2048]{1,0:T(8,128)(2,1)}, u32[]{:S(2)}) copy-start(bf16[128,2048]{1,0:T(8,128)(2,1)} %slice.171) | copy-start | bytes 1572868
  74.6 35.9 %collective-permute-start.9 = (bf16[128,4096]{1,0:T(8,128)(2,1)S(1)}, bf16[128,4096]{1,0:T(8,128)(2,1)S(1)}, u32[]{:S(2)}, u32[]{:S(2)}) collective-permute-start(bf16[128,4096]{1,0:T(8,128)(2,1)S(1)} %get-tuple-element.35), channel_id=1, source_target_pairs={{0,8},{8,16},{16,24},{25,17},{17,9},{9,1},{2,10},{10,18},{18,26},{... | collective-permute-start | bytes 3145736 | tf_op jit(solution)/shard_map/ppermute | solution.py:194
  79.0 28.0 %collective-permute-start.20 = (bf16[128,4096]{1,0:T(8,128)(2,1)S(1)}, bf16[128,4096]{1,0:T(8,128)(2,1)S(1)}, u32[]{:S(2)}, u32[]{:S(2)}) collective-permute-start(bf16[128,4096]{1,0:T(8,128)(2,1)S(1)} %get-tuple-element.42), channel_id=1, source_target_pairs={{1,9},{9,17},{17,25},{24,16},{16,8},{8,0},{3,11},{11,19},{19,27},{... | collective-permute-start | bytes 3145736 | tf_op jit(solution)/shard_map/ppermute | solution.py:194
  82.8 22.6 %copy-start.3 = (bf16[256,2048]{1,0:T(8,128)(2,1)S(1)}, bf16[256,2048]{1,0:T(8,128)(2,1)}, u32[]{:S(2)}) copy-start(bf16[256,2048]{1,0:T(8,128)(2,1)} %slice.183) | copy-start | bytes 3145732
  82.9 30.9 %collective-permute-start.7 = (bf16[128,4096]{1,0:T(8,128)(2,1)S(1)}, bf16[128,4096]{1,0:T(8,128)(2,1)S(1)}, u32[]{:S(2)}, u32[]{:S(2)}) collective-permute-start(bf16[128,4096]{1,0:T(8,128)(2,1)S(1)} %get-tuple-element.33), channel_id=1, source_target_pairs={{0,8},{8,16},{16,24},{25,17},{17,9},{9,1},{2,10},{10,18},{18,26},{... | collective-permute-start | bytes 3145736 | tf_op jit(solution)/shard_map/ppermute | solution.py:194
  105.5 5.0 %copy-start.7 = (bf16[256,4096]{1,0:T(8,128)(2,1)}, bf16[256,4096]{1,0:T(8,128)(2,1)S(1)}, u32[]{:S(2)}) copy-start(bf16[256,4096]{1,0:T(8,128)(2,1)S(1)} %collective-permute-done.1) | copy-start | bytes 6291460
  105.5 25.9 %collective-permute-start.13 = (bf16[256,2048]{1,0:T(8,128)(2,1)S(1)}, bf16[256,2048]{1,0:T(8,128)(2,1)S(1)}, u32[]{:S(2)}, u32[]{:S(2)}) collective-permute-start(bf16[256,2048]{1,0:T(8,128)(2,1)S(1)} %copy-done.3), channel_id=1, source_target_pairs={{0,4},{4,0},{1,5},{5,1},{2,6},{6,2},{3,7},{7,3},{8,12},{12,8},{9,1... | collective-permute-start | bytes 3145736 | tf_op jit(solution)/shard_map/ppermute | solution.py:198
  107.0 29.4 %collective-permute-start.21 = (bf16[128,4096]{1,0:T(8,128)(2,1)}, bf16[128,4096]{1,0:T(8,128)(2,1)S(1)}, u32[]{:S(2)}, u32[]{:S(2)}) collective-permute-start(bf16[128,4096]{1,0:T(8,128)(2,1)} %collective-permute-done.19), channel_id=1, source_target_pairs={{0,8},{8,16},{16,24},{25,17},{17,9},{9,1},{2,10},{10,18},{18,26},{... | collective-permute-start | bytes 3145736 | tf_op jit(solution)/shard_map/ppermute | solution.py:194
  110.7 20.7 %copy-start.6 = (bf16[256,1024]{1,0:T(8,128)(2,1)S(1)}, bf16[256,1024]{1,0:T(8,128)(2,1)}, u32[]{:S(2)}) copy-start(bf16[256,1024]{1,0:T(8,128)(2,1)} %slice.182) | copy-start | bytes 1572868
  110.7 26.9 %collective-permute-start.10 = (bf16[128,4096]{1,0:T(8,128)(2,1)S(1)}, bf16[128,4096]{1,0:T(8,128)(2,1)S(1)}, u32[]{:S(2)}, u32[]{:S(2)}) collective-permute-start(bf16[128,4096]{1,0:T(8,128)(2,1)S(1)} %get-tuple-element.36), channel_id=1, source_target_pairs={{1,9},{9,17},{17,25},{24,16},{16,8},{8,0},{3,11},{11,19},{19,27},{... | collective-permute-start | bytes 3145736 | tf_op jit(solution)/shard_map/ppermute | solution.py:194
  113.7 33.4 %collective-permute-start.23 = (bf16[128,4096]{1,0:T(8,128)(2,1)}, bf16[128,4096]{1,0:T(8,128)(2,1)S(1)}, u32[]{:S(2)}, u32[]{:S(2)}) collective-permute-start(bf16[128,4096]{1,0:T(8,128)(2,1)} %collective-permute-done.19), channel_id=1, source_target_pairs={{1,9},{9,17},{17,25},{24,16},{16,8},{8,0},{3,11},{11,19},{19,27},{... | collective-permute-start | bytes 3145736 | tf_op jit(solution)/shard_map/ppermute | solution.py:194
  131.4 16.4 %collective-permute-start.14 = (bf16[256,1024]{1,0:T(8,128)(2,1)S(1)}, bf16[256,1024]{1,0:T(8,128)(2,1)S(1)}, u32[]{:S(2)}, u32[]{:S(2)}) collective-permute-start(bf16[256,1024]{1,0:T(8,128)(2,1)S(1)} %copy-done.6), channel_id=1, source_target_pairs={{0,4},{4,0},{1,5},{5,1},{2,6},{6,2},{3,7},{7,3},{8,12},{12,8},{9,1... | collective-permute-start | bytes 1572872 | tf_op jit(solution)/shard_map/ppermute | solution.py:198
  136.4 23.7 %collective-permute-start.27 = (bf16[128,2048]{1,0:T(8,128)(2,1)S(1)}, bf16[128,2048]{1,0:T(8,128)(2,1)S(1)}, u32[]{:S(2)}, u32[]{:S(2)}) collective-permute-start(bf16[128,2048]{1,0:T(8,128)(2,1)S(1)} %get-tuple-element.52), channel_id=1, source_target_pairs={{1,9},{9,17},{17,25},{24,16},{16,8},{8,0},{3,11},{11,19},{19,27},{... | collective-permute-start | bytes 1572872 | tf_op jit(solution)/shard_map/ppermute | solution.py:194
  137.7 1.5 copy-start.8
  144.1 10.7 %collective-permute-start.11 = (f32[256,512]{0,1:T(8,128)S(1)}, f32[256,512]{0,1:T(8,128)S(1)}, u32[]{:S(2)}, u32[]{:S(2)}) collective-permute-start(f32[256,512]{0,1:T(8,128)S(1)} %slice_select_fusion.4), channel_id=1, source_target_pairs={{0,1},{1,0},{2,3},{3,2},{4,5},{5,4},{6,7},{7,6},{8,9},{9,8},{10,11... | collective-permute-start | bytes 1572872 | tf_op jit(solution)/shard_map/ppermute | solution.py:255
  147.9 4.2 %copy-start.5 = (bf16[256,2048]{1,0:T(8,128)(2,1)S(1)}, bf16[256,2048]{1,0:T(8,128)(2,1)}, u32[]{:S(2)}) copy-start(bf16[256,2048]{1,0:T(8,128)(2,1)} %get-tuple-element.39) | copy-start | bytes 3145732
  148.4 27.9 %collective-permute-start.24 = (bf16[128,4096]{1,0:T(8,128)(2,1)S(1)}, bf16[128,4096]{1,0:T(8,128)(2,1)S(1)}, u32[]{:S(2)}, u32[]{:S(2)}) collective-permute-start(bf16[128,4096]{1,0:T(8,128)(2,1)S(1)} %get-tuple-element.49), channel_id=1, source_target_pairs={{0,8},{8,16},{16,24},{25,17},{17,9},{9,1},{2,10},{10,18},{18,26},{... | collective-permute-start | bytes 3145736 | tf_op jit(solution)/shard_map/ppermute | solution.py:194
  152.2 25.5 %collective-permute-start.15 = (bf16[256,2048]{1,0:T(8,128)(2,1)S(1)}, bf16[256,2048]{1,0:T(8,128)(2,1)S(1)}, u32[]{:S(2)}, u32[]{:S(2)}) collective-permute-start(bf16[256,2048]{1,0:T(8,128)(2,1)S(1)} %copy-done.5), channel_id=1, source_target_pairs={{0,4},{4,0},{1,5},{5,1},{2,6},{6,2},{3,7},{7,3},{8,12},{12,8},{9,1... | collective-permute-start | bytes 3145736 | tf_op jit(solution)/shard_map/ppermute | solution.py:198
  154.9 15.7 %collective-permute-start.12 = (f32[256,512]{0,1:T(8,128)S(1)}, f32[256,512]{0,1:T(8,128)S(1)}, u32[]{:S(2)}, u32[]{:S(2)}) collective-permute-start(f32[256,512]{0,1:T(8,128)S(1)} %select_add_fusion), channel_id=1, source_target_pairs={{0,2},{2,0},{1,3},{3,1},{4,6},{6,4},{5,7},{7,5},{8,10},{10,8},{9,1... | collective-permute-start | bytes 1572872 | tf_op jit(solution)/shard_map/ppermute | solution.py:257
  156.5 13.5 %collective-permute-start.22 = (bf16[128,2048]{1,0:T(8,128)(2,1)S(1)}, bf16[128,2048]{1,0:T(8,128)(2,1)S(1)}, u32[]{:S(2)}, u32[]{:S(2)}) collective-permute-start(bf16[128,2048]{1,0:T(8,128)(2,1)S(1)} %get-tuple-element.46), channel_id=1, source_target_pairs={{0,8},{8,16},{16,24},{25,17},{17,9},{9,1},{2,10},{10,18},{18,26},{... | collective-permute-start | bytes 1572872 | tf_op jit(solution)/shard_map/ppermute | solution.py:194
  170.6 27.3 %collective-permute-start.28 = (bf16[128,2048]{1,0:T(8,128)(2,1)S(1)}, bf16[128,2048]{1,0:T(8,128)(2,1)S(1)}, u32[]{:S(2)}, u32[]{:S(2)}) collective-permute-start(bf16[128,2048]{1,0:T(8,128)(2,1)S(1)} %get-tuple-element.54), channel_id=1, source_target_pairs={{0,8},{8,16},{16,24},{25,17},{17,9},{9,1},{2,10},{10,18},{18,26},{... | collective-permute-start | bytes 1572872 | tf_op jit(solution)/shard_map/ppermute | solution.py:194
  175.0 26.7 %collective-permute-start.25 = (bf16[128,4096]{1,0:T(8,128)(2,1)S(1)}, bf16[128,4096]{1,0:T(8,128)(2,1)S(1)}, u32[]{:S(2)}, u32[]{:S(2)}) collective-permute-start(bf16[128,4096]{1,0:T(8,128)(2,1)S(1)} %get-tuple-element.50), channel_id=1, source_target_pairs={{1,9},{9,17},{17,25},{24,16},{16,8},{8,0},{3,11},{11,19},{19,27},{... | collective-permute-start | bytes 3145736 | tf_op jit(solution)/shard_map/ppermute | solution.py:194
  176.4 22.7 %collective-permute-start.30 = (bf16[128,2048]{1,0:T(8,128)(2,1)S(1)}, bf16[128,2048]{1,0:T(8,128)(2,1)S(1)}, u32[]{:S(2)}, u32[]{:S(2)}) collective-permute-start(bf16[128,2048]{1,0:T(8,128)(2,1)S(1)} %get-tuple-element.57), channel_id=1, source_target_pairs={{1,9},{9,17},{17,25},{24,16},{16,8},{8,0},{3,11},{11,19},{19,27},{... | collective-permute-start | bytes 1572872 | tf_op jit(solution)/shard_map/ppermute | solution.py:194
  177.7 15.6 %collective-permute-start.16 = (f32[256,512]{0,1:T(8,128)S(1)}, f32[256,512]{0,1:T(8,128)S(1)}, u32[]{:S(2)}, u32[]{:S(2)}) collective-permute-start(f32[256,512]{0,1:T(8,128)S(1)} %collective-permute-done.12), channel_id=1, source_target_pairs={{0,5},{1,4},{4,1},{5,0},{2,7},{3,6},{6,3},{7,2},{8,13},{9,12},{12,... | collective-permute-start | bytes 1572872 | tf_op jit(solution)/shard_map/ppermute | solution.py:260
  183.6 14.3 %copy-start.4 = (bf16[256,2048]{1,0:T(8,128)(2,1)S(1)}, bf16[256,2048]{1,0:T(8,128)(2,1)}, u32[]{:S(2)}) copy-start(bf16[256,2048]{1,0:T(8,128)(2,1)} %get-tuple-element.41) | copy-start | bytes 3145732
  193.4 22.0 %collective-permute-start.17 = (f32[256,1024]{0,1:T(8,128)S(1)}, f32[256,1024]{0,1:T(8,128)S(1)}, u32[]{:S(2)}, u32[]{:S(2)}) collective-permute-start(f32[256,1024]{0,1:T(8,128)S(1)} %bitcast.15), channel_id=1, source_target_pairs={{0,1},{1,0},{2,3},{3,2},{4,5},{5,4},{6,7},{7,6},{8,9},{9,8},{10,11... | collective-permute-start | bytes 3145736 | tf_op jit(solution)/shard_map/ppermute | solution.py:274
  194.4 21.0 %collective-permute-start.31 = (f32[256,768]{0,1:T(8,128)S(1)}, f32[256,768]{0,1:T(8,128)S(1)}, u32[]{:S(2)}, u32[]{:S(2)}) collective-permute-start(f32[256,768]{0,1:T(8,128)S(1)} %slice.196), channel_id=1, source_target_pairs={{0,8},{24,16},{1,9},{25,17},{2,10},{26,18},{3,11},{27,19},{4,12},{... | collective-permute-start | bytes 2359304 | tf_op jit(solution)/shard_map/ppermute | solution.py:266
  197.9 24.9 %collective-permute-start.18 = (bf16[256,2048]{1,0:T(8,128)(2,1)S(1)}, bf16[256,2048]{1,0:T(8,128)(2,1)S(1)}, u32[]{:S(2)}, u32[]{:S(2)}) collective-permute-start(bf16[256,2048]{1,0:T(8,128)(2,1)S(1)} %copy-done.4), channel_id=1, source_target_pairs={{0,4},{4,0},{1,5},{5,1},{2,6},{6,2},{3,7},{7,3},{8,12},{12,8},{9,1... | collective-permute-start | bytes 3145736 | tf_op jit(solution)/shard_map/ppermute | solution.py:198
  202.0 28.7 %collective-permute-start.26 = (bf16[128,4096]{1,0:T(8,128)(2,1)S(1)}, bf16[128,4096]{1,0:T(8,128)(2,1)S(1)}, u32[]{:S(2)}, u32[]{:S(2)}) collective-permute-start(bf16[128,4096]{1,0:T(8,128)(2,1)S(1)} %get-tuple-element.51), channel_id=1, source_target_pairs={{8,16},{16,24},{17,9},{9,1},{10,18},{18,26},{19,11},{11,3},{12,20}... | collective-permute-start | bytes 3145736 | tf_op jit(solution)/shard_map/ppermute | solution.py:194
  202.7 28.0 %collective-permute-start.29 = (bf16[128,4096]{1,0:T(8,128)(2,1)S(1)}, bf16[128,4096]{1,0:T(8,128)(2,1)S(1)}, u32[]{:S(2)}, u32[]{:S(2)}) collective-permute-start(bf16[128,4096]{1,0:T(8,128)(2,1)S(1)} %get-tuple-element.56), channel_id=1, source_target_pairs={{9,17},{17,25},{16,8},{8,0},{11,19},{19,27},{18,10},{10,2},{13,21}... | collective-permute-start | bytes 3145736 | tf_op jit(solution)/shard_map/ppermute | solution.py:194
  205.6 17.2 %copy-start.1 = (bf16[256,4096]{1,0:T(8,128)(2,1)S(1)}, bf16[256,4096]{1,0:T(8,128)(2,1)}, u32[]{:S(2)}) copy-start(bf16[256,4096]{1,0:T(8,128)(2,1)} %get-tuple-element.60) | copy-start | bytes 6291460
  205.6 17.2 %copy-start.9 = (f32[512,256]{0,1:T(8,128)S(1)}, f32[512,256]{0,1:T(8,128)}, u32[]{:S(2)}) copy-start(f32[512,256]{0,1:T(8,128)} %fusion.59) | copy-start | bytes 1572868
  215.4 19.9 %collective-permute-start.32 = (f32[256,768]{0,1:T(8,128)S(1)}, f32[256,768]{0,1:T(8,128)S(1)}, u32[]{:S(2)}, u32[]{:S(2)}) collective-permute-start(f32[256,768]{0,1:T(8,128)S(1)} %collective-permute-done.31), channel_id=1, source_target_pairs={{0,1},{1,0},{2,3},{3,2},{4,5},{5,4},{6,7},{7,6},{8,9},{9,8},{10,11... | collective-permute-start | bytes 2359304 | tf_op jit(solution)/shard_map/ppermute | solution.py:274
  236.3 1.2 collective-permute-start.33
  237.5 3.6 %collective-permute-start.34 = (f32[1024]{0:T(1024)S(1)}, f32[1024]{0:T(1024)S(1)}, u32[]{:S(2)}, u32[]{:S(2)}) collective-permute-start(f32[1024]{0:T(1024)S(1)} %fusion.129), channel_id=1, source_target_pairs={{0,2},{2,0},{1,3},{3,1},{4,6},{6,4},{5,7},{7,5},{8,10},{10,8},{9,1... | collective-permute-start | bytes 12296 | tf_op jit(solution)/shard_map/ppermute | solution.py:324
  241.1 3.7 %collective-permute-start.35 = (f32[256]{0:T(256)S(1)}, f32[256]{0:T(256)S(1)}, u32[]{:S(2)}, u32[]{:S(2)}) collective-permute-start(f32[256]{0:T(256)S(1)} %get-tuple-element.131), channel_id=1, source_target_pairs={{0,4},{4,0},{1,5},{5,1},{2,6},{6,2},{3,7},{7,3},{8,12},{12,8},{9,1... | collective-permute-start | bytes 3080 | tf_op jit(solution)/shard_map/ppermute | solution.py:327
  242.3 6.3 %collective-permute-start.37 = (f32[256]{0:T(256)S(1)}, f32[256]{0:T(256)S(1)}, u32[]{:S(2)}, u32[]{:S(2)}) collective-permute-start(f32[256]{0:T(256)S(1)} %get-tuple-element.132), channel_id=1, source_target_pairs={{8,4},{12,0},{16,28},{20,24},{9,5},{13,1},{17,29},{21,25},{10,6},{... | collective-permute-start | bytes 3080 | tf_op jit(solution)/shard_map/ppermute | solution.py:329
  243.6 5.8 %collective-permute-start.36 = (f32[256]{0:T(256)S(1)}, f32[256]{0:T(256)S(1)}, u32[]{:S(2)}, u32[]{:S(2)}) collective-permute-start(f32[256]{0:T(256)S(1)} %get-tuple-element.133), channel_id=1, source_target_pairs={{8,0},{16,24},{9,1},{17,25},{10,2},{18,26},{11,3},{19,27},{12,4},{... | collective-permute-start | bytes 3080 | tf_op jit(solution)/shard_map/ppermute | solution.py:327

commit v2 on v1

--- a/solution.py
+++ b/solution.py
@@ -226,12 +226,11 @@
     v_hand_a, v_hand_far = split(val_out, kept, hand)
     t_hand_a, t_hand_far = split(out_rows, kept, hand)
     t_kept_a, t_kept_far = split(out_rows, 0, kept)
-    v_hand_b = across(v_hand_far)
-    v_kept_b = across(v_kept_far)
-    t_own_b = across(own_rows, v_hand_b)
-    due[10] = t_own_b
-    t_hand_b1 = across(t_hand_far[:, : 2 * step], t_own_b)
-    t_hand_b2 = across(t_hand_far[:, 2 * step :], t_hand_b1)
+    t_own_b = across(own_rows)
+    v_hand_b = across(v_hand_far, t_own_b)
+    v_kept_b = across(v_kept_far, v_hand_b)
+    t_hand_b1 = across(t_hand_far[:, : 2 * step], v_kept_b)
+    t_hand_b2 = across(t_hand_far[:, 2 * step :], v_kept_b)
     due[14] = t_hand_b2
     w0 = wave(val_own, val_own)
     w1 = wave(v_kept_a, v_kept_a)
@@ -243,9 +242,12 @@
     w4 = wave(*last_hop((hand_1, hand_1), w2))
 
     t_own = jnp.concatenate((own_rows, t_own_b))
-    far_own = middle(w4)
-    cols = (val_own, jnp.where(low_end, far_own, w0[0]), middle(w2), jnp.where(high_end, far_own, w0[1]))
-    block = jnp.split(row_gram(t_own, jnp.concatenate(cols)), line, axis=1)
+    cols = (val_own, w0[0], middle(w2), w0[1])
+    part = row_gram(t_own, jnp.concatenate(cols))
+    block = jnp.split(part, line, axis=1)
+    far_part = row_gram(t_own, middle(w4))
+    block[1] = block[1] + jnp.where(low_end, far_part, 0.0)
+    block[3] = block[3] + jnp.where(high_end, far_part, 0.0)
     block[1], block[3] = jnp.where(core == 0, block[1], block[3]), jnp.where(core == 0, block[3], block[1])
     part = jnp.concatenate(block, axis=1)
 
@@ -257,12 +259,11 @@
     share = lax.ppermute(share, "section", SWAP)
     due[16] = share
     t_kept_b1 = across(t_kept_far[:, : 2 * step], t_hand_b2)
-    other = lax.ppermute(gate(share, t_kept_b1), ("pair", "tensor"), [(i, 3 - i) for i in range(4)])
+    t_kept_b2 = across(t_kept_far[:, 2 * step :], t_kept_b1)
+    other = lax.ppermute(share, ("pair", "tensor"), [(i, 3 - i) for i in range(4)])
     due[19] = other
-    t_kept_b2 = across(t_kept_far[:, 2 * step :], other)
     share = jnp.concatenate((share.reshape(rows, line, vals), other.reshape(rows, line, vals)), axis=2)
     share = share.reshape(rows, line * 2 * vals)
-    t_kept_b = jnp.concatenate((t_kept_b1, t_kept_b2), axis=1)
     far_share = lax.ppermute(share[:, 2 * vals :], "line", ends)
     w3 = wave(v_kept_b, v_kept_b)
     w5 = wave(*last_hop((hand_2, hand_2), [x[:, : 2 * step] for x in w6]))
@@ -287,34 +288,57 @@
         jnp.where(far_side, 0.0, far[1]),
     ]
 
-    def kept_gram(a, b):
-        return row_gram(t_kept, jnp.concatenate((a, b)))
-
-    t_kept = jnp.concatenate((t_kept_a, t_kept_b))
-    grams = [
-        kept_gram(v_kept_a, v_kept_b),
-        kept_gram(w1[0], w3[0]),
-        kept_gram(middle(w6), middle(w7)),
-        kept_gram(w1[1], w3[1]),
-    ]
-    last_gram = kept_gram(jnp.concatenate((middle(w5), middle(w9)), axis=1), middle(w8))
-    t_hand_b = jnp.concatenate((t_hand_b1, t_hand_b2), axis=1)
-    t_hand = jnp.concatenate((t_hand_a, t_hand_b))
-    far_1 = jnp.concatenate((stacked(other_way(w2), 2), stacked(other_way(w7), 2)))
-    far_2 = jnp.concatenate((stacked(other_way(w6)[:, : 2 * step], 2), stacked(other_way(w9), 2)))
+    full.append(jnp.where(end, jnp.where(far_side, full[3], full[1]), 0.0))
+
+    kept_rows = (
+        (v_kept_a, v_kept_b),
+        (w1[0], w3[0]),
+        (middle(w6), middle(w7)),
+        (w1[1], w3[1]),
+        (jnp.concatenate((middle(w5), middle(w9)), axis=1), middle(w8)),
+    )
+    kept_rows = [jnp.concatenate(x) for x in kept_rows]
     hand_rows = [(hand_1, hand_2), (w4[0], w5[0]), (middle(w8), middle(w9)), (w4[1], w5[1])]
-    unused = [None, high_end, end, low_end]
-    far_grams = []
-    for j, (one, two) in enumerate(hand_rows):
-        one, two = stacked(one, 2), stacked(two, 2)
-        gram = row_gram(t_hand[:, : 2 * step], one) + row_gram(t_hand[:, 2 * step :], two)
-        if j:
-            gram = jnp.where(unused[j], 0.0, gram)
-        grams[j] = grams[j] + gram
-        far_grams.append(row_gram(far_1, one) + row_gram(far_2, two))
-    last_inputs = jnp.where(end, jnp.where(far_side, full[3], full[1]), 0.0)
-    score = jnp.sum(sum(x * y for x, y in zip(full + [last_inputs], grams + [last_gram])), axis=1)
-    far_score = jnp.sum(sum(x * y for x, y in zip(far_full, far_grams)), axis=1)
+    hand_rows = [(stacked(one, 2), stacked(two, 2)) for one, two in hand_rows]
+    unused = (None, high_end, end, low_end)
+
+    def cut_gram(left, right, cuts):
+        total = 0.0
+        for x in left:
+            total = total + row_gram(x, right[:, cuts : cuts + x.shape[1]])
+            cuts += x.shape[1]
+        return total
+
+    def kept_scores(inputs, train, hand_train):
+        total = 0.0
+        for j, x in enumerate(inputs):
+            gram = cut_gram(train, kept_rows[j], 0)
+            if j < line:
+                other_gram = sum(row_gram(t, v) for t, v in zip(hand_train, hand_rows[j]))
+                gram = gram + (jnp.where(unused[j], 0.0, other_gram) if j else other_gram)
+            total = total + x * gram
+        return jnp.sum(total, axis=1)
+
+    def far_scores(inputs, train):
+        total = 0.0
+        for x, rows_j in zip(inputs, hand_rows):
+            total = total + x * sum(row_gram(t, v) for t, v in zip(train, rows_j))
+        return jnp.sum(total, axis=1)
+
+    def top(x):
+        return [y[:rows] for y in x]
+
+    def bottom(x):
+        return [y[rows:] for y in x]
+
+    hand_train = t_hand_a[:, : 2 * step], t_hand_a[:, 2 * step :]
+    far_a = stacked(other_way(w2), 2), stacked(other_way(w6)[:, : 2 * step], 2)
+    far_b = stacked(other_way(w7), 2), stacked(other_way(w9), 2)
+    score = jnp.concatenate((
+        kept_scores(top(full), (t_kept_a,), hand_train),
+        kept_scores(bottom(full), (t_kept_b1, t_kept_b2), (t_hand_b1, t_hand_b2)),
+    ))
+    far_score = jnp.concatenate((far_scores(top(far_full), far_a), far_scores(bottom(far_full), far_b)))
     return finish(score, far_score, rows, cores, core, ends)
 
 

time: 252 us -> 244 us (0.968)
  waiting for transfers between devices: 111 us -> 94.8 us
  matrix products: 26 us -> 35.4 us
  other arithmetic: 21.1 us -> 17.8 us
  starting transfers between devices: 79.2 us -> 82 us
    ppermute x7, waiting for transfers between devices: 41.1 us -> 22.1 us  [across(): return lax.ppermute(x if after is None else gate(x, after), 'pair', SWAP)]
    ppermute x20, waiting for transfers between devices: 42.8 us -> 60 us  [along(): sent.append(lax.ppermute(x, ('line', 'tensor'), pairs))]
    ppermute x1, waiting for transfers between devices: 9.72 us -> 0.01 us  [waves(): far_share = lax.ppermute(share[:, 2 * vals:], 'line', ends)]
    dot_general x22 -> x49, matrix products: 26 us -> 35.4 us  [row_gram(): lax.dot_general(left_rows, right_rows, (((1,), (1,)), ((), ())), preferre...]
    ppermute x1, waiting for transfers between devices: 9.64 us -> 3.36 us  [waves(): lax.ppermute(share, ('pair', 'tensor'), [(i, 3 - i) for i in range(4)])]
    select_n x3, other arithmetic: 5.38 us -> 0.67 us  [the longest x1 0.3 us: last_hop(): jnp.where(place == last - 1, held[0], x[0])]
    ppermute x1, starting transfers between devices: 3.9 us -> 0.07 us  [waves(): lax.ppermute(share, ('pair', 'tensor'), [(i, 3 - i) for i in range(4)])]
    unnamed x20 -> x34, local copies, waits for them, and re-layouts: 0.04 us -> 2.58 us
  transfers between devices with their start and end apart: 38 -> 38, of which waited for: 16 -> 17; matrix products, arithmetic and copies ran while one was open for 23% -> 24% of each run, Pallas kernels for 0% -> 0%
where the time goes in v2:
time: 244 us; the launch traced here: 243 us
  waiting for transfers between devices  94.8 us (39%)
  starting transfers between devices  82 us (34%)
  matrix products  35.4 us (15%)
  other arithmetic  17.8 us (7%)
  local copies, waits for them, and re-layouts  11.2 us (5%)
    ppermute x20, waiting for transfers between devices, along(): sent.append(lax.ppermute(x, ('line', 'tensor'), pairs))  60 us
    ppermute x20, starting transfers between devices, along(): sent.append(lax.ppermute(x, ('line', 'tensor'), pairs))  56.6 us
    dot_general x49, matrix products, row_gram(): lax.dot_general(left_rows, right_rows, (((1,), (1,)), ((), ())), preferre...  35.4 us
    ppermute x7, waiting for transfers between devices, across(): return lax.ppermute(x if after is None else gate(x, after), 'pair', SWAP)  22.1 us
    ppermute x7, starting transfers between devices, across(): return lax.ppermute(x if after is None else gate(x, after), 'pair', SWAP)  10.3 us
    select_n x4, other arithmetic, split(): return (jnp.where(side == 0, low, high), jnp.where(side == 0, high, low))  9.04 us
    ppermute x1, waiting for transfers between devices, finish(): mine = mine + lax.ppermute(far_b, ('line', 'pair'), slanted)  5.76 us
  transfers between devices with their start and end apart: 38, of which 17 were waited for; matrix products, arithmetic and copies ran while one was open for 24% of the time, Pallas kernels for 0%

profile of v2, /device:TPU:0, one launch (start us, length us, event | category | flops | bytes accessed | tf_op | source)
XLA Modules:
  0.0 243.0 jit_solution(2443750282158120674)
XLA Ops:
  1.9 6.6 %collective-permute-start.1 = (bf16[128,4096]{1,0:T(8,128)(2,1)}, bf16[128,4096]{1,0:T(8,128)(2,1)}, u32[]{:S(2)}, u32[]{:S(2)}) collective-permute-start(bf16[128,4096]{1,0:T(8,128)(2,1)} %bitcast.47), channel_id=1, source_target_pairs={{0,8},{8,16},{16,24},{25,17},{17,9},{9,1},{2,10},{10,18},{18,26},{... | collective-permute-start | bytes 3145736 | tf_op jit(solution)/shard_map/ppermute | solution.py:194
  8.6 3.1 %broadcast_select_fusion.8 = (bf16[128,4096]{1,0:T(8,128)(2,1)}, bf16[128,4096]{1,0:T(8,128)(2,1)}) fusion(pred[]{:T(512)S(6)} %eq.16, bf16[128,14336]{1,0:T(8,128)(2,1)} %bitcast.39), kind=kLoop, calls=%fused_computation.100 | loop fusion | flops 1048576 | bytes 4194305 | tf_op jit(solution)/shard_map/jit(_where)/select_n | solution.py:186
  11.7 4.1 %collective-permute-start.4 = (bf16[128,4096]{1,0:T(8,128)(2,1)}, bf16[128,4096]{1,0:T(8,128)(2,1)}, u32[]{:S(2)}, u32[]{:S(2)}) collective-permute-start(bf16[128,4096]{1,0:T(8,128)(2,1)} %get-tuple-element.33), channel_id=1, source_target_pairs={{0,8},{8,16},{16,24},{25,17},{17,9},{9,1},{2,10},{10,18},{18,26},{... | collective-permute-start | bytes 3145736 | tf_op jit(solution)/shard_map/ppermute | solution.py:194
  15.8 1.5 collective-permute-start
  17.3 3.2 %broadcast_select_fusion.2 = (bf16[256,3072]{1,0:T(8,128)(2,1)}, bf16[256,3072]{1,0:T(8,128)(2,1)S(1)}) fusion(pred[]{:T(512)S(6)} %eq.16, bf16[256,14336]{1,0:T(8,128)(2,1)} %bitcast.37), kind=kLoop, calls=%fused_computation.29 | loop fusion | flops 1572864 | bytes 6291457 | tf_op jit(solution)/shard_map/jit(_where)/select_n | solution.py:186
  20.8 1.6 fusion.99
  23.4 2.4 broadcast_select_fusion.24
  27.5 1.9 slice.306
  31.8 2.0 broadcast_select_fusion.12
  33.8 10.9 %collective-permute-done.4 = bf16[128,4096]{1,0:T(8,128)(2,1)} collective-permute-done((bf16[128,4096]{1,0:T(8,128)(2,1)}, bf16[128,4096]{1,0:T(8,128)(2,1)}, u32[]{:S(2)}, u32[]{:S(2)}) %collective-permute-start.4) | collective-permute-done | bytes 1048608 | tf_op jit(solution)/shard_map/ppermute | solution.py:194
  45.9 5.1 %collective-permute-start.3 = (bf16[128,4096]{1,0:T(8,128)(2,1)S(1)}, bf16[128,4096]{1,0:T(8,128)(2,1)S(1)}, u32[]{:S(2)}, u32[]{:S(2)}) collective-permute-start(bf16[128,4096]{1,0:T(8,128)(2,1)S(1)} %get-tuple-element.29), channel_id=1, source_target_pairs={{0,8},{8,16},{16,24},{25,17},{17,9},{9,1},{2,10},{10,18},{18,26},{... | collective-permute-start | bytes 3145736 | tf_op jit(solution)/shard_map/ppermute | solution.py:194
  51.0 1.5 constant_dynamic-update-slice_fusion.1
  52.5 9.3 %collective-permute-done = bf16[256,4096]{1,0:T(8,128)(2,1)} collective-permute-done((bf16[256,4096]{1,0:T(8,128)(2,1)}, bf16[256,4096]{1,0:T(8,128)(2,1)}, u32[]{:S(2)}, u32[]{:S(2)}) %collective-permute-start) | collective-permute-done | bytes 2097184 | tf_op jit(solution)/shard_map/ppermute | solution.py:198
  61.8 1.5 collective-permute-start.6
  63.3 3.7 %collective-permute-start.9 = (bf16[128,4096]{1,0:T(8,128)(2,1)S(1)}, bf16[128,4096]{1,0:T(8,128)(2,1)S(1)}, u32[]{:S(2)}, u32[]{:S(2)}) collective-permute-start(bf16[128,4096]{1,0:T(8,128)(2,1)S(1)} %get-tuple-element.34), channel_id=1, source_target_pairs={{0,8},{8,16},{16,24},{25,17},{17,9},{9,1},{2,10},{10,18},{18,26},{... | collective-permute-start | bytes 3145736 | tf_op jit(solution)/shard_map/ppermute | solution.py:194
  67.2 5.9 %collective-permute-done.3 = bf16[128,4096]{1,0:T(8,128)(2,1)S(1)} collective-permute-done((bf16[128,4096]{1,0:T(8,128)(2,1)S(1)}, bf16[128,4096]{1,0:T(8,128)(2,1)S(1)}, u32[]{:S(2)}, u32[]{:S(2)}) %collective-permute-start.3) | collective-permute-done | bytes 1048608 | tf_op jit(solution)/shard_map/ppermute | solution.py:194
  74.4 2.3 collective-permute-done.6
  77.7 5.1 %collective-permute-start.7 = (bf16[128,4096]{1,0:T(8,128)(2,1)S(1)}, bf16[128,4096]{1,0:T(8,128)(2,1)S(1)}, u32[]{:S(2)}, u32[]{:S(2)}) collective-permute-start(bf16[128,4096]{1,0:T(8,128)(2,1)S(1)} %get-tuple-element.32), channel_id=1, source_target_pairs={{0,8},{8,16},{16,24},{25,17},{17,9},{9,1},{2,10},{10,18},{18,26},{... | collective-permute-start | bytes 3145736 | tf_op jit(solution)/shard_map/ppermute | solution.py:194
  82.8 1.6 collective-permute-start.15
  86.7 5.5 %fusion = f32[512,512]{0,1:T(8,128)} fusion(bf16[128,4096]{1,0:T(8,128)(2,1)} %collective-permute-done.2, bf16[128,4096]{1,0:T(8,128)(2,1)S(1)} %get-tuple-element.80, bf16[128,4096]{1,0:T(8,128)(2,1)} %collective-permute-done.1, bf16[128,4096]{1,0:T(8,128)(2,1)S(1)} %bitcast.48, bf16[256,4096]{1,0:T(8,128)(2,1)} %collective-permute-done, ...), kind=kOutput, calls=%fused_computation.1 | convolution fusion | flops 2172649472 | bytes 9437184 | tf_op jit(solution)/shard_map/dot_general | solution.py:11
  93.6 8.2 %collective-permute-done.16 = bf16[128,4096]{1,0:T(8,128)(2,1)S(1)} collective-permute-done((bf16[128,4096]{1,0:T(8,128)(2,1)S(1)}, bf16[128,4096]{1,0:T(8,128)(2,1)S(1)}, u32[]{:S(2)}, u32[]{:S(2)}) %collective-permute-start.16) | collective-permute-done | bytes 1048608 | tf_op jit(solution)/shard_map/ppermute | solution.py:194
  103.1 3.1 %collective-permute-done.15 = bf16[128,4096]{1,0:T(8,128)(2,1)} collective-permute-done((bf16[128,4096]{1,0:T(8,128)(2,1)S(1)}, bf16[128,4096]{1,0:T(8,128)(2,1)}, u32[]{:S(2)}, u32[]{:S(2)}) %collective-permute-start.15) | collective-permute-done | bytes 1048608 | tf_op jit(solution)/shard_map/ppermute | solution.py:198
  106.3 4.3 %collective-permute-start.17 = (bf16[128,4096]{1,0:T(8,128)(2,1)}, bf16[128,4096]{1,0:T(8,128)(2,1)S(1)}, u32[]{:S(2)}, u32[]{:S(2)}) collective-permute-start(bf16[128,4096]{1,0:T(8,128)(2,1)} %collective-permute-done.15), channel_id=1, source_target_pairs={{0,8},{8,16},{16,24},{25,17},{17,9},{9,1},{2,10},{10,18},{18,26},{... | collective-permute-start | bytes 3145736 | tf_op jit(solution)/shard_map/ppermute | solution.py:194
  110.6 1.6 collective-permute-start.21
  114.2 3.0 %fusion.22 = f32[256,256]{0,1:T(8,128)} fusion(f32[256,256]{0,1:T(8,128)S(1)} %convolution_add_fusion.22, bf16[256,4096]{1,0:T(8,128)(2,1)S(1)} %get-tuple-element.61, bf16[128,4096]{1,0:T(8,128)(2,1)} %collective-permute-done.15, bf16[128,4096]{1,0:T(8,128)(2,1)} %get-tuple-element.33), kind=kOutput, calls=%fused_computation.66 | convolution fusion | flops 541130752 | bytes 4718592 | tf_op jit(solution)/shard_map/dot_general | solution.py:11
  117.3 7.0 %collective-permute-done.10 = bf16[128,4096]{1,0:T(8,128)(2,1)S(1)} collective-permute-done((bf16[128,4096]{1,0:T(8,128)(2,1)S(1)}, bf16[128,4096]{1,0:T(8,128)(2,1)S(1)}, u32[]{:S(2)}, u32[]{:S(2)}) %collective-permute-start.10) | collective-permute-done | bytes 1048608 | tf_op jit(solution)/shard_map/ppermute | solution.py:194
  124.3 3.4 %fusion.109 = (f32[512,128]{0,1:T(8,128)S(1)}, f32[512,128]{0,1:T(8,128)S(1)}, f32[512,128]{0,1:T(8,128)S(1)}, f32[512,128]{0,1:T(8,128)S(1)}) fusion(f32[512,512]{0,1:T(8,128)} %fusion, pred[]{:T(512)S(6)} %eq.15, pred[]{:T(512)S(6)} %eq.17, pred[]{:T(512)S(6)} %eq.14, bf16[128,4096]{1,0:T(8,128)(2,1)S(1)} %collective-permute-done.7, ...), kind=kOutput, calls=%fused_computation.239 | convolution fusion | flops 546177024 | bytes 8388612 | tf_op jit(solution)/shard_map/dot_general | solution.py:11
  129.0 2.1 collective-permute-start.29
  131.6 1.6 collective-permute-start.12
  133.2 1.7 collective-permute-done.17
  134.8 5.8 %collective-permute-start.18 = (bf16[128,2048]{1,0:T(8,128)(2,1)S(1)}, bf16[128,2048]{1,0:T(8,128)(2,1)S(1)}, u32[]{:S(2)}, u32[]{:S(2)}) collective-permute-start(bf16[128,2048]{1,0:T(8,128)(2,1)S(1)} %get-tuple-element.40), channel_id=1, source_target_pairs={{0,8},{8,16},{16,24},{25,17},{17,9},{9,1},{2,10},{10,18},{18,26},{... | collective-permute-start | bytes 1572872 | tf_op jit(solution)/shard_map/ppermute | solution.py:194
  140.6 7.4 %collective-permute-done.19 = bf16[256,2048]{1,0:T(8,128)(2,1)S(1)} collective-permute-done((bf16[256,2048]{1,0:T(8,128)(2,1)S(1)}, bf16[256,2048]{1,0:T(8,128)(2,1)S(1)}, u32[]{:S(2)}, u32[]{:S(2)}) %collective-permute-start.19) | collective-permute-done | bytes 1048608 | tf_op jit(solution)/shard_map/ppermute | solution.py:198
  150.1 4.6 %collective-permute-start.22 = (bf16[128,4096]{1,0:T(8,128)(2,1)S(1)}, bf16[128,4096]{1,0:T(8,128)(2,1)S(1)}, u32[]{:S(2)}, u32[]{:S(2)}) collective-permute-start(bf16[128,4096]{1,0:T(8,128)(2,1)S(1)} %get-tuple-element.45), channel_id=1, source_target_pairs={{0,8},{8,16},{16,24},{25,17},{17,9},{9,1},{2,10},{10,18},{18,26},{... | collective-permute-start | bytes 3145736 | tf_op jit(solution)/shard_map/ppermute | solution.py:194
  159.9 4.9 %collective-permute-done.25 = bf16[128,2048]{1,0:T(8,128)(2,1)S(1)} collective-permute-done((bf16[128,2048]{1,0:T(8,128)(2,1)S(1)}, bf16[128,2048]{1,0:T(8,128)(2,1)S(1)}, u32[]{:S(2)}, u32[]{:S(2)}) %collective-permute-start.25) | collective-permute-done | bytes 524320 | tf_op jit(solution)/shard_map/ppermute | solution.py:194
  165.3 3.4 %collective-permute-start.26 = (bf16[128,2048]{1,0:T(8,128)(2,1)S(1)}, bf16[128,2048]{1,0:T(8,128)(2,1)S(1)}, u32[]{:S(2)}, u32[]{:S(2)}) collective-permute-start(bf16[128,2048]{1,0:T(8,128)(2,1)S(1)} %get-tuple-element.50), channel_id=1, source_target_pairs={{0,8},{8,16},{16,24},{25,17},{17,9},{9,1},{2,10},{10,18},{18,26},{... | collective-permute-start | bytes 1572872 | tf_op jit(solution)/shard_map/ppermute | solution.py:194
  168.7 1.6 collective-permute-start.30
  173.0 3.4 %collective-permute-done.13 = f32[256,512]{0,1:T(8,128)S(1)} collective-permute-done((f32[256,512]{0,1:T(8,128)S(1)}, f32[256,512]{0,1:T(8,128)S(1)}, u32[]{:S(2)}, u32[]{:S(2)}) %collective-permute-start.13) | collective-permute-done | bytes 524320 | tf_op jit(solution)/shard_map/ppermute | solution.py:263
  177.7 4.3 %collective-permute-start.31 = (f32[256,768]{0,1:T(8,128)S(1)}, f32[256,768]{0,1:T(8,128)S(1)}, u32[]{:S(2)}, u32[]{:S(2)}) collective-permute-start(f32[256,768]{0,1:T(8,128)S(1)} %slice.335), channel_id=1, source_target_pairs={{0,8},{24,16},{1,9},{25,17},{2,10},{26,18},{3,11},{27,19},{4,12},{... | collective-permute-start | bytes 2359304 | tf_op jit(solution)/shard_map/ppermute | solution.py:267
  184.4 17.6 %collective-permute-done.28 = bf16[128,2048]{1,0:T(8,128)(2,1)S(1)} collective-permute-done((bf16[128,2048]{1,0:T(8,128)(2,1)S(1)}, bf16[128,2048]{1,0:T(8,128)(2,1)S(1)}, u32[]{:S(2)}, u32[]{:S(2)}) %collective-permute-start.28) | collective-permute-done | bytes 524320 | tf_op jit(solution)/shard_map/ppermute | solution.py:194
  202.0 1.5 collective-permute-start.27
  206.4 1.7 fusion.32
  208.6 2.2 collective-permute-start.32
  211.2 1.7 fusion.18
  215.5 3.9 %collective-permute-done.27 = bf16[128,4096]{1,0:T(8,128)(2,1)S(1)} collective-permute-done((bf16[128,4096]{1,0:T(8,128)(2,1)S(1)}, bf16[128,4096]{1,0:T(8,128)(2,1)S(1)}, u32[]{:S(2)}, u32[]{:S(2)}) %collective-permute-start.27) | collective-permute-done | bytes 1048608 | tf_op jit(solution)/shard_map/ppermute | solution.py:194
  227.8 1.6 collective-permute-start.34
  229.4 2.1 collective-permute-done.34
  234.1 1.6 collective-permute-start.35
  235.7 5.8 %collective-permute-done.37 = f32[256]{0:T(256)S(1)} collective-permute-done((f32[256]{0:T(256)S(1)}, f32[256]{0:T(256)S(1)}, u32[]{:S(2)}, u32[]{:S(2)}) %collective-permute-start.37) | collective-permute-done | bytes 1056 | tf_op jit(solution)/shard_map/ppermute | solution.py:353
  (163 shorter events, 51.9 us)
Async XLA Ops:
  0.6 31.1 %collective-permute-start.2 = (bf16[128,4096]{1,0:T(8,128)(2,1)}, bf16[128,4096]{1,0:T(8,128)(2,1)}, u32[]{:S(2)}, u32[]{:S(2)}) collective-permute-start(bf16[128,4096]{1,0:T(8,128)(2,1)} %bitcast.46), channel_id=1, source_target_pairs={{1,9},{9,17},{17,25},{24,16},{16,8},{8,0},{3,11},{11,19},{19,27},{... | collective-permute-start | bytes 3145736 | tf_op jit(solution)/shard_map/ppermute | solution.py:194
  1.9 28.5 %collective-permute-start.1 = (bf16[128,4096]{1,0:T(8,128)(2,1)}, bf16[128,4096]{1,0:T(8,128)(2,1)}, u32[]{:S(2)}, u32[]{:S(2)}) collective-permute-start(bf16[128,4096]{1,0:T(8,128)(2,1)} %bitcast.47), channel_id=1, source_target_pairs={{0,8},{8,16},{16,24},{25,17},{17,9},{9,1},{2,10},{10,18},{18,26},{... | collective-permute-start | bytes 3145736 | tf_op jit(solution)/shard_map/ppermute | solution.py:194
  8.6 12.0 %copy-start = (bf16[1,256,14336]{2,1,0:T(8,128)(2,1)S(1)}, bf16[1,256,14336]{2,1,0:T(8,128)(2,1)}, u32[]{:S(2)}) copy-start(bf16[1,256,14336]{2,1,0:T(8,128)(2,1)} %param.5) | copy-start | bytes 22020100
  11.7 32.9 %collective-permute-start.4 = (bf16[128,4096]{1,0:T(8,128)(2,1)}, bf16[128,4096]{1,0:T(8,128)(2,1)}, u32[]{:S(2)}, u32[]{:S(2)}) collective-permute-start(bf16[128,4096]{1,0:T(8,128)(2,1)} %get-tuple-element.33), channel_id=1, source_target_pairs={{0,8},{8,16},{16,24},{25,17},{17,9},{9,1},{2,10},{10,18},{18,26},{... | collective-permute-start | bytes 3145736 | tf_op jit(solution)/shard_map/ppermute | solution.py:194
  15.8 46.0 %collective-permute-start = (bf16[256,4096]{1,0:T(8,128)(2,1)}, bf16[256,4096]{1,0:T(8,128)(2,1)}, u32[]{:S(2)}, u32[]{:S(2)}) collective-permute-start(bf16[256,4096]{1,0:T(8,128)(2,1)} %bitcast.43), channel_id=1, source_target_pairs={{0,4},{4,0},{1,5},{5,1},{2,6},{6,2},{3,7},{7,3},{8,12},{12,8},{9,1... | collective-permute-start | bytes 6291464 | tf_op jit(solution)/shard_map/ppermute | solution.py:198
  20.5 5.3 %copy-start.1 = (bf16[256,3072]{1,0:T(8,128)(2,1)}, bf16[256,3072]{1,0:T(8,128)(2,1)S(1)}, u32[]{:S(2)}) copy-start(bf16[256,3072]{1,0:T(8,128)(2,1)S(1)} %get-tuple-element.64) | copy-start | bytes 4718596
  30.5 32.8 %collective-permute-start.8 = (bf16[128,4096]{1,0:T(8,128)(2,1)}, bf16[128,4096]{1,0:T(8,128)(2,1)S(1)}, u32[]{:S(2)}, u32[]{:S(2)}) collective-permute-start(bf16[128,4096]{1,0:T(8,128)(2,1)} %get-tuple-element.33), channel_id=1, source_target_pairs={{1,9},{9,17},{17,25},{24,16},{16,8},{8,0},{3,11},{11,19},{19,27},{... | collective-permute-start | bytes 3145736 | tf_op jit(solution)/shard_map/ppermute | solution.py:194
  33.8 28.0 %copy-start.11 = (bf16[128,3072]{1,0:T(8,128)(2,1)S(1)}, bf16[128,3072]{1,0:T(8,128)(2,1)}, u32[]{:S(2)}) copy-start(bf16[128,3072]{1,0:T(8,128)(2,1)} %get-tuple-element.31) | copy-start | bytes 2359300
  44.6 32.1 %collective-permute-start.5 = (bf16[128,4096]{1,0:T(8,128)(2,1)S(1)}, bf16[128,4096]{1,0:T(8,128)(2,1)S(1)}, u32[]{:S(2)}, u32[]{:S(2)}) collective-permute-start(bf16[128,4096]{1,0:T(8,128)(2,1)S(1)} %get-tuple-element.30), channel_id=1, source_target_pairs={{1,9},{9,17},{17,25},{24,16},{16,8},{8,0},{3,11},{11,19},{19,27},{... | collective-permute-start | bytes 3145736 | tf_op jit(solution)/shard_map/ppermute | solution.py:194
  45.9 27.2 %collective-permute-start.3 = (bf16[128,4096]{1,0:T(8,128)(2,1)S(1)}, bf16[128,4096]{1,0:T(8,128)(2,1)S(1)}, u32[]{:S(2)}, u32[]{:S(2)}) collective-permute-start(bf16[128,4096]{1,0:T(8,128)(2,1)S(1)} %get-tuple-element.29), channel_id=1, source_target_pairs={{0,8},{8,16},{16,24},{25,17},{17,9},{9,1},{2,10},{10,18},{18,26},{... | collective-permute-start | bytes 3145736 | tf_op jit(solution)/shard_map/ppermute | solution.py:194
  61.8 14.9 %collective-permute-start.6 = (bf16[128,3072]{1,0:T(8,128)(2,1)S(1)}, bf16[128,3072]{1,0:T(8,128)(2,1)S(1)}, u32[]{:S(2)}, u32[]{:S(2)}) collective-permute-start(bf16[128,3072]{1,0:T(8,128)(2,1)S(1)} %copy-done.11), channel_id=1, source_target_pairs={{0,4},{4,0},{1,5},{5,1},{2,6},{6,2},{3,7},{7,3},{8,12},{12,8},{9,1... | collective-permute-start | bytes 2359304 | tf_op jit(solution)/shard_map/ppermute | solution.py:198
  63.3 13.5 %copy-start.4 = (bf16[128,2048]{1,0:T(8,128)(2,1)S(1)}, bf16[128,2048]{1,0:T(8,128)(2,1)}, u32[]{:S(2)}) copy-start(bf16[128,2048]{1,0:T(8,128)(2,1)} %slice.287) | copy-start | bytes 1572868
  63.3 29.0 %collective-permute-start.9 = (bf16[128,4096]{1,0:T(8,128)(2,1)S(1)}, bf16[128,4096]{1,0:T(8,128)(2,1)S(1)}, u32[]{:S(2)}, u32[]{:S(2)}) collective-permute-start(bf16[128,4096]{1,0:T(8,128)(2,1)S(1)} %get-tuple-element.34), channel_id=1, source_target_pairs={{0,8},{8,16},{16,24},{25,17},{17,9},{9,1},{2,10},{10,18},{18,26},{... | collective-permute-start | bytes 3145736 | tf_op jit(solution)/shard_map/ppermute | solution.py:194
  73.1 28.7 %collective-permute-start.16 = (bf16[128,4096]{1,0:T(8,128)(2,1)S(1)}, bf16[128,4096]{1,0:T(8,128)(2,1)S(1)}, u32[]{:S(2)}, u32[]{:S(2)}) collective-permute-start(bf16[128,4096]{1,0:T(8,128)(2,1)S(1)} %get-tuple-element.37), channel_id=1, source_target_pairs={{1,9},{9,17},{17,25},{24,16},{16,8},{8,0},{3,11},{11,19},{19,27},{... | collective-permute-start | bytes 3145736 | tf_op jit(solution)/shard_map/ppermute | solution.py:194
  76.7 6.1 %copy-start.6 = (bf16[128,4096]{1,0:T(8,128)(2,1)S(1)}, bf16[128,4096]{1,0:T(8,128)(2,1)}, u32[]{:S(2)}) copy-start(bf16[128,4096]{1,0:T(8,128)(2,1)} %get-tuple-element.36) | copy-start | bytes 3145732
  77.7 6.8 %copy-start.2 = (bf16[256,3072]{1,0:T(8,128)(2,1)S(1)}, bf16[256,3072]{1,0:T(8,128)(2,1)}, u32[]{:S(2)}) copy-start(bf16[256,3072]{1,0:T(8,128)(2,1)} %copy-done.1) | copy-start | bytes 4718596
  77.7 6.8 %copy-start.7 = (bf16[128,1024]{1,0:T(8,128)(2,1)S(1)}, bf16[128,1024]{1,0:T(8,128)(2,1)}, u32[]{:S(2)}) copy-start(bf16[128,1024]{1,0:T(8,128)(2,1)} %slice.298) | copy-start | bytes 786436
  77.7 35.0 %collective-permute-start.7 = (bf16[128,4096]{1,0:T(8,128)(2,1)S(1)}, bf16[128,4096]{1,0:T(8,128)(2,1)S(1)}, u32[]{:S(2)}, u32[]{:S(2)}) collective-permute-start(bf16[128,4096]{1,0:T(8,128)(2,1)S(1)} %get-tuple-element.32), channel_id=1, source_target_pairs={{0,8},{8,16},{16,24},{25,17},{17,9},{9,1},{2,10},{10,18},{18,26},{... | collective-permute-start | bytes 3145736 | tf_op jit(solution)/shard_map/ppermute | solution.py:194
  82.8 23.4 %collective-permute-start.15 = (bf16[128,4096]{1,0:T(8,128)(2,1)S(1)}, bf16[128,4096]{1,0:T(8,128)(2,1)}, u32[]{:S(2)}, u32[]{:S(2)}) collective-permute-start(bf16[128,4096]{1,0:T(8,128)(2,1)S(1)} %copy-done.6), channel_id=1, source_target_pairs={{0,4},{4,0},{1,5},{5,1},{2,6},{6,2},{3,7},{7,3},{8,12},{12,8},{9,1... | collective-permute-start | bytes 3145736 | tf_op jit(solution)/shard_map/ppermute | solution.py:198
  92.3 32.0 %collective-permute-start.10 = (bf16[128,4096]{1,0:T(8,128)(2,1)S(1)}, bf16[128,4096]{1,0:T(8,128)(2,1)S(1)}, u32[]{:S(2)}, u32[]{:S(2)}) collective-permute-start(bf16[128,4096]{1,0:T(8,128)(2,1)S(1)} %get-tuple-element.35), channel_id=1, source_target_pairs={{1,9},{9,17},{17,25},{24,16},{16,8},{8,0},{3,11},{11,19},{19,27},{... | collective-permute-start | bytes 3145736 | tf_op jit(solution)/shard_map/ppermute | solution.py:194
  102.6 8.0 %copy-start.12 = (bf16[256,1024]{1,0:T(8,128)(2,1)S(1)}, bf16[256,1024]{1,0:T(8,128)(2,1)}, u32[]{:S(2)}) copy-start(bf16[256,1024]{1,0:T(8,128)(2,1)} %slice.306) | copy-start | bytes 1572868
  102.7 9.5 %copy-start.8 = (bf16[256,2048]{1,0:T(8,128)(2,1)S(1)}, bf16[256,2048]{1,0:T(8,128)(2,1)}, u32[]{:S(2)}) copy-start(bf16[256,2048]{1,0:T(8,128)(2,1)} %slice.303) | copy-start | bytes 3145732
  106.3 28.6 %collective-permute-start.17 = (bf16[128,4096]{1,0:T(8,128)(2,1)}, bf16[128,4096]{1,0:T(8,128)(2,1)S(1)}, u32[]{:S(2)}, u32[]{:S(2)}) collective-permute-start(bf16[128,4096]{1,0:T(8,128)(2,1)} %collective-permute-done.15), channel_id=1, source_target_pairs={{0,8},{8,16},{16,24},{25,17},{17,9},{9,1},{2,10},{10,18},{18,26},{... | collective-permute-start | bytes 3145736 | tf_op jit(solution)/shard_map/ppermute | solution.py:194
  110.6 17.4 %collective-permute-start.21 = (bf16[256,1024]{1,0:T(8,128)(2,1)S(1)}, bf16[256,1024]{1,0:T(8,128)(2,1)S(1)}, u32[]{:S(2)}, u32[]{:S(2)}) collective-permute-start(bf16[256,1024]{1,0:T(8,128)(2,1)S(1)} %copy-done.12), channel_id=1, source_target_pairs={{0,4},{4,0},{1,5},{5,1},{2,6},{6,2},{3,7},{7,3},{8,12},{12,8},{9,1... | collective-permute-start | bytes 1572872 | tf_op jit(solution)/shard_map/ppermute | solution.py:198
  112.2 35.8 %collective-permute-start.19 = (bf16[256,2048]{1,0:T(8,128)(2,1)S(1)}, bf16[256,2048]{1,0:T(8,128)(2,1)S(1)}, u32[]{:S(2)}, u32[]{:S(2)}) collective-permute-start(bf16[256,2048]{1,0:T(8,128)(2,1)S(1)} %copy-done.8), channel_id=1, source_target_pairs={{0,4},{4,0},{1,5},{5,1},{2,6},{6,2},{3,7},{7,3},{8,12},{12,8},{9,1... | collective-permute-start | bytes 3145736 | tf_op jit(solution)/shard_map/ppermute | solution.py:198
  112.7 36.7 %collective-permute-start.20 = (bf16[128,4096]{1,0:T(8,128)(2,1)}, bf16[128,4096]{1,0:T(8,128)(2,1)S(1)}, u32[]{:S(2)}, u32[]{:S(2)}) collective-permute-start(bf16[128,4096]{1,0:T(8,128)(2,1)} %collective-permute-done.15), channel_id=1, source_target_pairs={{1,9},{9,17},{17,25},{24,16},{16,8},{8,0},{3,11},{11,19},{19,27},{... | collective-permute-start | bytes 3145736 | tf_op jit(solution)/shard_map/ppermute | solution.py:194
  117.2 7.1 %copy-start.14 = (bf16[1,256,4096]{2,1,0:T(8,128)(2,1)S(1)}, bf16[1,256,4096]{2,1,0:T(8,128)(2,1)}, u32[]{:S(2)}) copy-start(bf16[1,256,4096]{2,1,0:T(8,128)(2,1)} %param.4) | copy-start | bytes 6291460
  127.8 3.6 %collective-permute-start.11 = (f32[256,512]{0,1:T(8,128)S(1)}, f32[256,512]{0,1:T(8,128)S(1)}, u32[]{:S(2)}, u32[]{:S(2)}) collective-permute-start(f32[256,512]{0,1:T(8,128)S(1)} %slice_select_fusion.4), channel_id=1, source_target_pairs={{0,1},{1,0},{2,3},{3,2},{4,5},{5,4},{6,7},{7,6},{8,9},{9,8},{10,11... | collective-permute-start | bytes 1572872 | tf_op jit(solution)/shard_map/ppermute | solution.py:257
  129.0 39.7 %collective-permute-start.29 = (bf16[256,2048]{1,0:T(8,128)(2,1)S(1)}, bf16[256,2048]{1,0:T(8,128)(2,1)S(1)}, u32[]{:S(2)}, u32[]{:S(2)}) collective-permute-start(bf16[256,2048]{1,0:T(8,128)(2,1)S(1)} %copy-done.10), channel_id=1, source_target_pairs={{0,4},{4,0},{1,5},{5,1},{2,6},{6,2},{3,7},{7,3},{8,12},{12,8},{9,1... | collective-permute-start | bytes 3145736 | tf_op jit(solution)/shard_map/ppermute | solution.py:198
  131.6 26.6 %collective-permute-start.12 = (f32[256,512]{0,1:T(8,128)S(1)}, f32[256,512]{0,1:T(8,128)S(1)}, u32[]{:S(2)}, u32[]{:S(2)}) collective-permute-start(f32[256,512]{0,1:T(8,128)S(1)} %select_add_fusion), channel_id=1, source_target_pairs={{0,2},{2,0},{1,3},{3,1},{4,6},{6,4},{5,7},{7,5},{8,10},{10,8},{9,1... | collective-permute-start | bytes 1572872 | tf_op jit(solution)/shard_map/ppermute | solution.py:259
  134.8 20.4 %collective-permute-start.18 = (bf16[128,2048]{1,0:T(8,128)(2,1)S(1)}, bf16[128,2048]{1,0:T(8,128)(2,1)S(1)}, u32[]{:S(2)}, u32[]{:S(2)}) collective-permute-start(bf16[128,2048]{1,0:T(8,128)(2,1)S(1)} %get-tuple-element.40), channel_id=1, source_target_pairs={{0,8},{8,16},{16,24},{25,17},{17,9},{9,1},{2,10},{10,18},{18,26},{... | collective-permute-start | bytes 1572872 | tf_op jit(solution)/shard_map/ppermute | solution.py:194
  148.0 16.7 %collective-permute-start.25 = (bf16[128,2048]{1,0:T(8,128)(2,1)S(1)}, bf16[128,2048]{1,0:T(8,128)(2,1)S(1)}, u32[]{:S(2)}, u32[]{:S(2)}) collective-permute-start(bf16[128,2048]{1,0:T(8,128)(2,1)S(1)} %get-tuple-element.48), channel_id=1, source_target_pairs={{1,9},{9,17},{17,25},{24,16},{16,8},{8,0},{3,11},{11,19},{19,27},{... | collective-permute-start | bytes 1572872 | tf_op jit(solution)/shard_map/ppermute | solution.py:194
  150.1 27.6 %collective-permute-start.22 = (bf16[128,4096]{1,0:T(8,128)(2,1)S(1)}, bf16[128,4096]{1,0:T(8,128)(2,1)S(1)}, u32[]{:S(2)}, u32[]{:S(2)}) collective-permute-start(bf16[128,4096]{1,0:T(8,128)(2,1)S(1)} %get-tuple-element.45), channel_id=1, source_target_pairs={{0,8},{8,16},{16,24},{25,17},{17,9},{9,1},{2,10},{10,18},{18,26},{... | collective-permute-start | bytes 3145736 | tf_op jit(solution)/shard_map/ppermute | solution.py:194
  156.0 26.0 %collective-permute-start.23 = (bf16[128,4096]{1,0:T(8,128)(2,1)S(1)}, bf16[128,4096]{1,0:T(8,128)(2,1)S(1)}, u32[]{:S(2)}, u32[]{:S(2)}) collective-permute-start(bf16[128,4096]{1,0:T(8,128)(2,1)S(1)} %get-tuple-element.46), channel_id=1, source_target_pairs={{1,9},{9,17},{17,25},{24,16},{16,8},{8,0},{3,11},{11,19},{19,27},{... | collective-permute-start | bytes 3145736 | tf_op jit(solution)/shard_map/ppermute | solution.py:194
  158.1 18.3 %collective-permute-start.13 = (f32[256,512]{0,1:T(8,128)S(1)}, f32[256,512]{0,1:T(8,128)S(1)}, u32[]{:S(2)}, u32[]{:S(2)}) collective-permute-start(f32[256,512]{0,1:T(8,128)S(1)} %collective-permute-done.12), channel_id=1, source_target_pairs={{0,5},{1,4},{4,1},{5,0},{2,7},{3,6},{6,3},{7,2},{8,13},{9,12},{12,... | collective-permute-start | bytes 1572872 | tf_op jit(solution)/shard_map/ppermute | solution.py:263
  165.3 18.3 %collective-permute-start.26 = (bf16[128,2048]{1,0:T(8,128)(2,1)S(1)}, bf16[128,2048]{1,0:T(8,128)(2,1)S(1)}, u32[]{:S(2)}, u32[]{:S(2)}) collective-permute-start(bf16[128,2048]{1,0:T(8,128)(2,1)S(1)} %get-tuple-element.50), channel_id=1, source_target_pairs={{0,8},{8,16},{16,24},{25,17},{17,9},{9,1},{2,10},{10,18},{18,26},{... | collective-permute-start | bytes 1572872 | tf_op jit(solution)/shard_map/ppermute | solution.py:194
  168.7 37.7 %collective-permute-start.30 = (bf16[256,2048]{1,0:T(8,128)(2,1)S(1)}, bf16[256,2048]{1,0:T(8,128)(2,1)S(1)}, u32[]{:S(2)}, u32[]{:S(2)}) collective-permute-start(bf16[256,2048]{1,0:T(8,128)(2,1)S(1)} %copy-done.9), channel_id=1, source_target_pairs={{0,4},{4,0},{1,5},{5,1},{2,6},{6,2},{3,7},{7,3},{8,12},{12,8},{9,1... | collective-permute-start | bytes 3145736 | tf_op jit(solution)/shard_map/ppermute | solution.py:198
  176.5 38.5 %collective-permute-start.14 = (f32[256,1024]{0,1:T(8,128)S(1)}, f32[256,1024]{0,1:T(8,128)S(1)}, u32[]{:S(2)}, u32[]{:S(2)}) collective-permute-start(f32[256,1024]{0,1:T(8,128)S(1)} %bitcast.36), channel_id=1, source_target_pairs={{0,1},{1,0},{2,3},{3,2},{4,5},{5,4},{6,7},{7,6},{8,9},{9,8},{10,11... | collective-permute-start | bytes 3145736 | tf_op jit(solution)/shard_map/ppermute | solution.py:275
  177.7 30.9 %collective-permute-start.31 = (f32[256,768]{0,1:T(8,128)S(1)}, f32[256,768]{0,1:T(8,128)S(1)}, u32[]{:S(2)}, u32[]{:S(2)}) collective-permute-start(f32[256,768]{0,1:T(8,128)S(1)} %slice.335), channel_id=1, source_target_pairs={{0,8},{24,16},{1,9},{25,17},{2,10},{26,18},{3,11},{27,19},{4,12},{... | collective-permute-start | bytes 2359304 | tf_op jit(solution)/shard_map/ppermute | solution.py:267
  182.0 20.0 %collective-permute-start.28 = (bf16[128,2048]{1,0:T(8,128)(2,1)S(1)}, bf16[128,2048]{1,0:T(8,128)(2,1)S(1)}, u32[]{:S(2)}, u32[]{:S(2)}) collective-permute-start(bf16[128,2048]{1,0:T(8,128)(2,1)S(1)} %get-tuple-element.53), channel_id=1, source_target_pairs={{1,9},{9,17},{17,25},{24,16},{16,8},{8,0},{3,11},{11,19},{19,27},{... | collective-permute-start | bytes 1572872 | tf_op jit(solution)/shard_map/ppermute | solution.py:194
  183.6 31.9 %collective-permute-start.24 = (bf16[128,4096]{1,0:T(8,128)(2,1)S(1)}, bf16[128,4096]{1,0:T(8,128)(2,1)S(1)}, u32[]{:S(2)}, u32[]{:S(2)}) collective-permute-start(bf16[128,4096]{1,0:T(8,128)(2,1)S(1)} %get-tuple-element.47), channel_id=1, source_target_pairs={{8,16},{16,24},{17,9},{9,1},{10,18},{18,26},{19,11},{11,3},{12,20}... | collective-permute-start | bytes 3145736 | tf_op jit(solution)/shard_map/ppermute | solution.py:194
  202.0 17.4 %collective-permute-start.27 = (bf16[128,4096]{1,0:T(8,128)(2,1)S(1)}, bf16[128,4096]{1,0:T(8,128)(2,1)S(1)}, u32[]{:S(2)}, u32[]{:S(2)}) collective-permute-start(bf16[128,4096]{1,0:T(8,128)(2,1)S(1)} %get-tuple-element.52), channel_id=1, source_target_pairs={{9,17},{17,25},{16,8},{8,0},{11,19},{19,27},{18,10},{10,2},{13,21}... | collective-permute-start | bytes 3145736 | tf_op jit(solution)/shard_map/ppermute | solution.py:194
  208.6 16.7 %collective-permute-start.32 = (f32[256,768]{0,1:T(8,128)S(1)}, f32[256,768]{0,1:T(8,128)S(1)}, u32[]{:S(2)}, u32[]{:S(2)}) collective-permute-start(f32[256,768]{0,1:T(8,128)S(1)} %collective-permute-done.31), channel_id=1, source_target_pairs={{0,1},{1,0},{2,3},{3,2},{4,5},{5,4},{6,7},{7,6},{8,9},{9,8},{10,11... | collective-permute-start | bytes 2359304 | tf_op jit(solution)/shard_map/ppermute | solution.py:275
  226.6 1.2 collective-permute-start.33
  227.8 3.7 %collective-permute-start.34 = (f32[1024]{0:T(1024)S(1)}, f32[1024]{0:T(1024)S(1)}, u32[]{:S(2)}, u32[]{:S(2)}) collective-permute-start(f32[1024]{0:T(1024)S(1)} %fusion.85), channel_id=1, source_target_pairs={{0,2},{2,0},{1,3},{3,1},{4,6},{6,4},{5,7},{7,5},{8,10},{10,8},{9,1... | collective-permute-start | bytes 12296 | tf_op jit(solution)/shard_map/ppermute | solution.py:348
  231.5 9.9 %collective-permute-start.37 = (f32[256]{0:T(256)S(1)}, f32[256]{0:T(256)S(1)}, u32[]{:S(2)}, u32[]{:S(2)}) collective-permute-start(f32[256]{0:T(256)S(1)} %get-tuple-element.143), channel_id=1, source_target_pairs={{8,4},{12,0},{16,28},{20,24},{9,5},{13,1},{17,29},{21,25},{10,6},{... | collective-permute-start | bytes 3080 | tf_op jit(solution)/shard_map/ppermute | solution.py:353
  232.8 9.0 %collective-permute-start.36 = (f32[256]{0:T(256)S(1)}, f32[256]{0:T(256)S(1)}, u32[]{:S(2)}, u32[]{:S(2)}) collective-permute-start(f32[256]{0:T(256)S(1)} %get-tuple-element.144), channel_id=1, source_target_pairs={{8,0},{16,24},{9,1},{17,25},{10,2},{18,26},{11,3},{19,27},{12,4},{... | collective-permute-start | bytes 3080 | tf_op jit(solution)/shard_map/ppermute | solution.py:351
  234.1 7.7 %collective-permute-start.35 = (f32[256]{0:T(256)S(1)}, f32[256]{0:T(256)S(1)}, u32[]{:S(2)}, u32[]{:S(2)}) collective-permute-start(f32[256]{0:T(256)S(1)} %get-tuple-element.142), channel_id=1, source_target_pairs={{0,4},{4,0},{1,5},{5,1},{2,6},{6,2},{3,7},{7,3},{8,12},{12,8},{9,1... | collective-permute-start | bytes 3080 | tf_op jit(solution)/shard_map/ppermute | solution.py:351
  (7 other events, 17.4 us)
